TPU v7x, 32 devices: a whole 2x2x4 slice. The times are simulated.
32 devices in a mesh: req: 8 (over z, x), tp: 4 (over y, core).
Axes of the slice: x: 2, y: 2, z: 4, core: 2. Of those that a mesh axis runs over, the one named last changes fastest.
Arguments:
- hidden_in: bfloat16 [16, 512, 1280], P('req'), may hold values from -6 to 6
- lengths: int32 [16], P('req'), may hold values from 128 to 512, as said below
- attn_gain: float32 [1280], replicated, may hold values from 0.1 to 1.9
- mlp_gain: float32 [1280], replicated, may hold values from 0.1 to 1.9
- q_master: float32 [1280, 1280], P(('req', 'tp')), may hold values from -1 to 1
- k_master: float32 [1280, 320], P(('req', 'tp')), may hold values from -1 to 1
- trainer_value_weight: float32 [1280, 320], P(('req', 'tp')), may hold values from -0.15625 to 0.15625
- o_master: float32 [1280, 1280], P(('req', 'tp')), may hold values from -0.15625 to 0.15625
- gate_master: float32 [1280, 3584], P(('req', 'tp')), may hold values from -0.15625 to 0.15625
- up_master: float32 [1280, 3584], P(('req', 'tp')), may hold values from -0.15625 to 0.15625
- down_master: float32 [3584, 1280], P(('req', 'tp')), may hold values from -0.09375 to 0.09375
Outputs:
- hidden_out: bfloat16 [16, 512, 1280], P('req')
- kv_cache: bfloat16 [16, 512, 640], P('req')
Inputs may be any that keep to these rules, and one draw needn't show every extreme that they name: `lengths`: each prompt has at least a quarter of 512 real tokens; in every draw some prompt has exactly 512.
All inputs are finite; a program needn't handle non-finite values.
Results may differ from a plain program's by a relative error of at most 0.012.
Values may be sent and summed in bfloat16 or wider, within the bound.
A program may use at most 192 MiB of HBM per device.

v0:
```python
import math

import jax
import jax.numpy as jnp
from jax import lax
from jax.sharding import PartitionSpec as P

QUERY_HEADS = 20
KEY_VALUE_HEADS = 5
HEAD_DIM = 64


def rms_norm(field, gain_vec):
    scale = lax.rsqrt(jnp.mean(field * field, axis=-1, keepdims=True) + 1e-05)
    return (field * scale * gain_vec).astype(jnp.bfloat16)


def rope_tables(sequence_length, head_size):
    half_width = head_size // 2
    positions = jnp.arange(sequence_length, dtype=jnp.float32)[:, None]
    frequency = jnp.exp(
        -math.log(10000.0) * (2.0 * jnp.arange(half_width, dtype=jnp.float32) / head_size)
    )
    angles = positions * frequency[None, :]
    return (jnp.cos(angles), jnp.sin(angles))


def rotate(field, cosine_table, sine_table):
    half_width = field.shape[-1] // 2
    first_half = field[..., :half_width]
    second_half = field[..., half_width:]
    cos_b = cosine_table[:, None, :]
    sin_b = sine_table[:, None, :]
    return jnp.concatenate(
        [first_half * cos_b - second_half * sin_b, second_half * cos_b + first_half * sin_b],
        axis=-1,
    )


def local(
    hidden_in,
    lengths,
    attn_gain,
    mlp_gain,
    q_master,
    k_master,
    trainer_value_weight,
    o_master,
    gate_master,
    up_master,
    down_master,
):
    tp_count = lax.axis_size("tp")
    tensor_shard_index = lax.axis_index("tp")
    q_cast = q_master.astype(jnp.bfloat16)
    k_cast = k_master.astype(jnp.bfloat16)
    v_cast = trainer_value_weight.astype(jnp.bfloat16)
    o_cast = o_master.astype(jnp.bfloat16)
    gate_cast = gate_master.astype(jnp.bfloat16)
    up_cast = up_master.astype(jnp.bfloat16)
    down_cast = down_master.astype(jnp.bfloat16)
    q_cols = q_master.shape[1] // tp_count
    ff_cols = gate_master.shape[1] // tp_count
    q_full, key_weight, value_weight, o_full, gate_full, up_full, down_full = (
        lax.all_gather(q_cast, ("req", "tp"), axis=0, tiled=True),
        lax.all_gather(k_cast, ("req", "tp"), axis=0, tiled=True),
        lax.all_gather(v_cast, ("req", "tp"), axis=0, tiled=True),
        lax.all_gather(o_cast, ("req", "tp"), axis=0, tiled=True),
        lax.all_gather(gate_cast, ("req", "tp"), axis=0, tiled=True),
        lax.all_gather(up_cast, ("req", "tp"), axis=0, tiled=True),
        lax.all_gather(down_cast, ("req", "tp"), axis=0, tiled=True),
    )
    query_weight = lax.dynamic_slice_in_dim(q_full, tensor_shard_index * q_cols, q_cols, 1)
    gate_weight = lax.dynamic_slice_in_dim(gate_full, tensor_shard_index * ff_cols, ff_cols, 1)
    up_weight = lax.dynamic_slice_in_dim(up_full, tensor_shard_index * ff_cols, ff_cols, 1)
    out_weight = lax.dynamic_slice_in_dim(o_full, tensor_shard_index * q_cols, q_cols, 0)
    down_weight = lax.dynamic_slice_in_dim(down_full, tensor_shard_index * ff_cols, ff_cols, 0)
    prompt_batch, sequence_length, model_width = hidden_in.shape
    tok_rows = prompt_batch * sequence_length
    flat_rows = hidden_in.reshape(tok_rows, model_width).astype(jnp.float32)
    normalized_input = rms_norm(flat_rows, attn_gain)
    local_heads = query_weight.shape[1] // HEAD_DIM
    queries = jnp.dot(normalized_input, query_weight, preferred_element_type=jnp.float32).reshape(
        prompt_batch, sequence_length, local_heads, HEAD_DIM
    )
    key_rows = jnp.dot(normalized_input, key_weight, preferred_element_type=jnp.float32).reshape(
        prompt_batch, sequence_length, KEY_VALUE_HEADS, HEAD_DIM
    )
    value_rows = jnp.dot(
        normalized_input, value_weight, preferred_element_type=jnp.float32
    ).reshape(prompt_batch, sequence_length, KEY_VALUE_HEADS, HEAD_DIM)
    cosine_table, sine_table = rope_tables(sequence_length, HEAD_DIM)
    q_rot = rotate(queries, cosine_table, sine_table).astype(jnp.bfloat16)
    rotated_keys = rotate(key_rows, cosine_table, sine_table).astype(jnp.bfloat16)
    value_halves = value_rows.astype(jnp.bfloat16)
    kv_cache = jnp.concatenate(
        [
            rotated_keys.reshape(prompt_batch, sequence_length, KEY_VALUE_HEADS * HEAD_DIM),
            value_halves.reshape(prompt_batch, sequence_length, KEY_VALUE_HEADS * HEAD_DIM),
        ],
        axis=2,
    )
    owner_shards = (
        tensor_shard_index * local_heads + jnp.arange(local_heads, dtype=jnp.int32)
    ) // (QUERY_HEADS // KEY_VALUE_HEADS)
    selector_mask = (
        owner_shards[:, None] == jnp.arange(KEY_VALUE_HEADS, dtype=jnp.int32)[None, :]
    ).astype(jnp.bfloat16)
    k_local = jnp.einsum(
        "pshd,gh->psgd", rotated_keys, selector_mask, preferred_element_type=jnp.float32
    ).astype(jnp.bfloat16)
    v_local = jnp.einsum(
        "pshd,gh->psgd", value_halves, selector_mask, preferred_element_type=jnp.float32
    ).astype(jnp.bfloat16)
    scores = jnp.einsum(
        "pqhd,pkhd->phqk", q_rot, k_local, preferred_element_type=jnp.float32
    ) / math.sqrt(HEAD_DIM)
    row_index = jnp.arange(sequence_length, dtype=jnp.int32)[:, None]
    col_index = jnp.arange(sequence_length, dtype=jnp.int32)[None, :]
    allowed = (col_index <= row_index)[None, None] & (
        col_index[None, None] < lengths[:, None, None, None]
    )
    scores = jnp.where(allowed, scores, -1e30)
    highest = jnp.max(scores, axis=-1, keepdims=True)
    expo = jnp.exp(scores - highest)
    weight_table = (expo / jnp.sum(expo, axis=-1, keepdims=True)).astype(jnp.bfloat16)
    attended = (
        jnp.einsum("phqk,pkhd->pqhd", weight_table, v_local, preferred_element_type=jnp.float32)
        .astype(jnp.bfloat16)
        .reshape(tok_rows, local_heads * HEAD_DIM)
    )
    attn_total = lax.psum(
        jnp.dot(attended, out_weight, preferred_element_type=jnp.float32).astype(jnp.bfloat16), "tp"
    ).astype(jnp.float32)
    middle = flat_rows + attn_total
    normed_rows = rms_norm(middle, mlp_gain)
    gate_val = jnp.dot(normed_rows, gate_weight, preferred_element_type=jnp.float32)
    up_val = jnp.dot(normed_rows, up_weight, preferred_element_type=jnp.float32)
    hidden_ff = (jax.nn.silu(gate_val) * up_val).astype(jnp.bfloat16)
    ffn_total = lax.psum(
        jnp.dot(hidden_ff, down_weight, preferred_element_type=jnp.float32).astype(jnp.bfloat16),
        "tp",
    ).astype(jnp.float32)
    result = (middle + ffn_total).astype(jnp.bfloat16)
    return (result.reshape(prompt_batch, sequence_length, model_width), kv_cache)


def solution(mesh):
    placed = (
        P("req", None, None),
        P("req"),
        P(),
        P(),
        P(("req", "tp"), None),
        P(("req", "tp"), None),
        P(("req", "tp"), None),
        P(("req", "tp"), None),
        P(("req", "tp"), None),
        P(("req", "tp"), None),
        P(("req", "tp"), None),
    )
    return jax.shard_map(
        local,
        mesh=mesh,
        in_specs=placed,
        out_specs=(P("req", None, None), P("req", None, None)),
        check_vma=False,
    )
```

profile of v0, /device:TPU:13, one launch (start us, length us, event | category | flops | bytes accessed | tf_op | source)
XLA Modules:
  0.0 530.9 jit_solution(15078366842234620480)
XLA Ops:
  7.2 0.0 copy-start.6
  7.2 0.0 copy-start
  7.2 0.0 all-gather.6.cloned.1.call-start
  7.2 1.7 convert_element_type.101
  9.0 0.0 all-gather.6.cloned.1.call-update
  9.0 0.0 all-gather.8.cloned.1.call-start
  9.0 1.6 convert_element_type.109
  10.6 0.0 all-gather.8.cloned.1.call-update
  10.6 0.0 all-reduce.3.cloned.1.call-start
  10.7 0.8 convert_element_type.102
  11.5 37.9 %all_gather.23 = bf16[1280,320]{1,0:T(8,128)(2,1)} all-gather(bf16[40,320]{1,0:T(8,128)(2,1)S(1)} %convert_element_type.102), channel_id=1, replica_groups=mesh['req'=8,'tp'=4] {'req','tp'}, dimensions={0}, use_global_device_ids=true | all-gather | bytes 844800 | tf_op jit(solution)/shard_map/all_gather | solution.py:66
  49.4 1.5 copy.21
  51.0 46.7 %all_gather.21 = bf16[1280,320]{1,0:T(8,128)(2,1)} all-gather(bf16[40,320]{1,0:T(8,128)(2,1)S(1)} %convert_element_type.97), channel_id=1, replica_groups=mesh['req'=8,'tp'=4] {'req','tp'}, dimensions={0}, use_global_device_ids=true | all-gather | bytes 844800 | tf_op jit(solution)/shard_map/all_gather | solution.py:67
  97.7 2.2 copy.19
  99.9 0.1 iota_compare_fusion
  100.0 0.6 multiply_reduce_fusion.1
  100.6 0.3 fusion.33
  100.9 0.0 copy-start.8
  100.9 1.1 fusion.27
  102.1 0.0 copy-start.3
  102.1 0.2 multiply_subtract_fusion
  102.4 0.0 copy-done.8
  102.4 0.1 iota_compare_fusion.1
  102.4 1.1 broadcast_and_fusion
  103.6 1.5 fusion.18
  105.1 1.2 convolution_convert_fusion.2
  106.3 0.9 copy-done.2
  107.2 1.5 fusion.20
  108.7 2.5 dynamic-slice_bitcast_fusion
  111.2 2.2 copy.20
  113.5 2.3 fusion.29
  115.8 1.1 subtract_convert_fusion
  116.9 9.6 %fusion.52 = (f32[2,5,512]{2,1,0:T(8,128)S(1)}, f32[2,5,512,512]{2,3,1,0:T(8,128)}) fusion(pred[2,512,512]{1,2,0:T(8,128)(4,1)} %broadcast_and_fusion, bf16[2,512,5,32]{1,3,2,0:T(8,128)(2,1)} %get-tuple-element.3, bf16[2,512,5,32]{1,3,2,0:T(8,128)(2,1)} %get-tuple-element.2, bf16[5,2,512,64]{2,0,3,1:T(8,128)(2,1)} %fusion.18), kind=kOutput, calls=%fused_computation.74 | convolution fusion | flops 347341312 | bytes 12341248 | tf_op jit(solution)/shard_map/sub | solution.py:125
  126.5 5.4 %fusion.15 = bf16[2,512,5,64]{1,3,2,0:T(8,128)(2,1)S(1)} fusion(f32[2,5,512,512]{2,3,1,0:T(8,128)} %get-tuple-element.9, f32[2,5,512]{2,1,0:T(8,128)S(1)} %get-tuple-element.8, bf16[5,2,512,64]{2,0,3,1:T(8,128)(2,1)} %fusion.20), kind=kOutput, calls=%fused_computation.30 | convolution fusion | flops 341114880 | bytes 11816960 | tf_op jit(solution)/shard_map/phqk,pkhd->pqhd/dot_general | solution.py:128
  131.9 0.7 copy.23
  132.6 0.9 copy.33
  133.5 0.9 all-gather.8.cloned.1.call-done
  134.4 4.4 convolution_convert_fusion.1
  138.8 0.0 all-reduce.3.cloned.1.call-update
  138.9 0.0 all-gather.12.cloned.1.call-start
  138.9 1.8 convert_element_type.114
  140.7 0.0 all-gather.12.cloned.1.call-update
  140.7 0.0 copy-start.7
  140.8 0.0 all-gather.10.cloned.1.call-start
  140.8 1.8 convert_element_type.113
  142.6 0.0 all-gather.10.cloned.1.call-update
  142.6 0.0 all-gather.14.cloned.1.call-start
  142.7 1.8 convert_element_type.116
  144.5 0.0 all-gather.14.cloned.1.call-update
  144.5 0.3 all-reduce.5.cloned.1.call-start
  144.8 56.1 %all-reduce.3.cloned.1.call-done = bf16[1024,1280]{1,0:T(8,128)(2,1)} async-done(((bf16[1024,1280]{1,0:T(8,128)(2,1)}), bf16[1024,1280]{1,0:T(8,128)(2,1)}) %all-reduce.3.cloned.1.call-update) | async-done | bytes 2621456 | tf_op jit(solution)/shard_map/psum | solution.py:132
  200.9 2.8 multiply_reduce_fusion
  203.8 2.5 multiply_convert_fusion
  206.2 79.3 %all-gather.12.cloned.1.call-done = bf16[1280,3584]{1,0:T(8,128)(2,1)} async-done(((bf16[40,3584]{1,0:T(8,128)(2,1)}), bf16[1280,3584]{1,0:T(8,128)(2,1)}) %all-gather.12.cloned.1.call-update) | async-done | bytes 9175056 | tf_op jit(solution)/shard_map/all_gather | solution.py:70
  285.5 7.2 %fusion.8 = f32[1024,896]{1,0:T(8,128)} fusion(bf16[1024,1280]{1,0:T(8,128)(2,1)} %multiply_convert_fusion, bf16[1280,3584]{1,0:T(8,128)(2,1)} %all-gather.12.cloned.1.call-done, s32[]{:T(128)S(6)} %select_n.25), kind=kOutput, calls=%fused_computation.20 | convolution fusion | flops 2348810240 | bytes 8585220 | tf_op jit(solution)/shard_map/dot_general | solution.py:138
  292.7 74.9 %all-gather.10.cloned.1.call-done = bf16[1280,3584]{1,0:T(8,128)(2,1)} async-done(((bf16[40,3584]{1,0:T(8,128)(2,1)}), bf16[1280,3584]{1,0:T(8,128)(2,1)}) %all-gather.10.cloned.1.call-update) | async-done | bytes 9175056 | tf_op jit(solution)/shard_map/all_gather | solution.py:69
  367.6 82.5 %all-gather.14.cloned.1.call-done = bf16[3584,1280]{1,0:T(8,128)(2,1)} async-done(((bf16[112,1280]{1,0:T(8,128)(2,1)}), bf16[3584,1280]{1,0:T(8,128)(2,1)}) %all-gather.14.cloned.1.call-update) | async-done | bytes 9175056 | tf_op jit(solution)/shard_map/all_gather | solution.py:71
  450.1 11.4 %convolution_convert_fusion = bf16[1024,1280]{1,0:T(8,128)(2,1)} fusion(bf16[3584,1280]{1,0:T(8,128)(2,1)} %all-gather.14.cloned.1.call-done, s32[]{:T(128)S(6)} %select_n.25, f32[1024,896]{1,0:T(8,128)} %fusion.8, bf16[1024,1280]{1,0:T(8,128)(2,1)} %multiply_convert_fusion, bf16[1280,3584]{1,0:T(8,128)(2,1)} %all-gather.10.cloned.1.call-done), kind=kOutput, calls=%fused_computation.15 | convolution fusion | flops 4704436224 | bytes 13501440 | tf_op jit(solution)/shard_map/dot_general | solution.py:141
  461.5 0.0 all-reduce.5.cloned.1.call-update
  461.6 1.2 copy.24
  462.7 1.4 copy.25
  464.2 2.6 pad_maximum_fusion
  466.8 52.3 %all-reduce.5.cloned.1.call-done = bf16[1024,1280]{1,0:T(8,128)(2,1)} async-done(((bf16[1024,1280]{1,0:T(8,128)(2,1)}), bf16[1024,1280]{1,0:T(8,128)(2,1)}) %all-reduce.5.cloned.1.call-update) | async-done | bytes 2621456 | tf_op jit(solution)/shard_map/psum | solution.py:140
  519.1 5.0 add_convert_fusion
  (20 shorter events, 0.1 us)
Async XLA Ops:
  7.2 43.8 %copy-start.6 = (f32[40,320]{1,0:T(8,128)S(1)}, f32[40,320]{1,0:T(8,128)}, u32[]{:S(2)}) copy-start(f32[40,320]{1,0:T(8,128)} %param.17) | copy-start | bytes 153604
  7.2 92.8 %copy-start = (bf16[2,512,1280]{2,1,0:T(8,128)(2,1)S(1)}, bf16[2,512,1280]{2,1,0:T(8,128)(2,1)}, u32[]{:S(2)}) copy-start(bf16[2,512,1280]{2,1,0:T(8,128)(2,1)} %param.11) | copy-start | bytes 7864324
  7.2 101.5 %all-gather.6.cloned.1.call-start = ((), (), s32[]{:S(2)}) async-start(), calls=%async_computation | async-start | bytes 3379200 | tf_op jit(solution)/shard_map/all_gather | solution.py:65
  9.0 125.4 %all-gather.8.cloned.1.call-start = ((), (), s32[]{:S(2)}) async-start(), calls=%async_computation.1 | async-start | bytes 3379200 | tf_op jit(solution)/shard_map/all_gather | solution.py:68
  10.6 190.3 %all-reduce.3.cloned.1.call-start = ((), (), s32[]{:S(2)}) async-start(), calls=%async_computation.2 | async-start | bytes 5242880 | tf_op jit(solution)/shard_map/psum | solution.py:132
  49.4 51.5 %copy-start.9 = (f32[1280]{0:T(1024)S(1)}, f32[1280]{0:T(1024)}, u32[]{:S(2)}) copy-start(f32[1280]{0:T(1024)} %param.13) | copy-start | bytes 15364
  100.9 1.2 copy-start.4
  100.9 1.4 copy-start.8
  102.1 3.0 copy-start.3
  106.3 0.9 copy-start.2
  113.4 2.3 copy-start.5
  138.9 146.7 %all-gather.12.cloned.1.call-start = ((), (), s32[]{:S(2)}) async-start(), calls=%async_computation.4 | async-start | bytes 9461760 | tf_op jit(solution)/shard_map/all_gather | solution.py:70
  140.7 63.0 %copy-start.7 = (f32[1280]{0:T(1024)S(1)}, f32[1280]{0:T(1024)}, u32[]{:S(2)}) copy-start(f32[1280]{0:T(1024)} %param.14) | copy-start | bytes 15364
  140.8 226.9 %all-gather.10.cloned.1.call-start = ((), (), s32[]{:S(2)}) async-start(), calls=%async_computation.3 | async-start | bytes 9461760 | tf_op jit(solution)/shard_map/all_gather | solution.py:69
  142.6 307.5 %all-gather.14.cloned.1.call-start = ((), (), s32[]{:S(2)}) async-start(), calls=%async_computation.5 | async-start | bytes 9461760 | tf_op jit(solution)/shard_map/all_gather | solution.py:71
  144.5 374.6 %all-reduce.5.cloned.1.call-start = ((), (), s32[]{:S(2)}) async-start(), calls=%async_computation.6 | async-start | bytes 5242880 | tf_op jit(solution)/shard_map/psum | solution.py:140
  200.9 2.8 copy-start.1
Sparse Core Ops, SparseCore 0:
  10.9 62.3 all-gather.5
  76.0 58.3 all-gather.7
  139.0 61.8 all-reduce.2
  203.6 81.8 all-gather.11
  288.2 79.3 all-gather.9
  370.9 79.2 all-gather.13
  461.7 57.3 all-reduce.4
where the time goes:
time: 534 us; the launch traced here: 531 us
  waiting for transfers between devices  346 us (65%)
  blocking collectives  84.6 us (16%)
  matrix products  45.7 us (9%)
  other arithmetic  26 us (5%)
  between operations  14.4 us (3%)
  local copies, waits for them, and re-layouts  13.6 us (3%)
    all_gather x1, waiting for transfers between devices, local(): lax.all_gather(down_cast, ('req', 'tp'), axis=0, tiled=True)  82.5 us
    all_gather x1, waiting for transfers between devices, local(): lax.all_gather(up_cast, ('req', 'tp'), axis=0, tiled=True)  79.3 us
    all_gather x1, waiting for transfers between devices, local(): lax.all_gather(gate_cast, ('req', 'tp'), axis=0, tiled=True)  74.9 us
    psum x1, waiting for transfers between devices, local(): lax.psum(jnp.dot(attended, out_weight, preferred_element_type=jnp.float32...  56.1 us
    psum x1, waiting for transfers between devices, local(): lax.psum(jnp.dot(hidden_ff, down_weight, preferred_element_type=jnp.float...  52.3 us
    all_gather x1, blocking collectives, local(): lax.all_gather(v_cast, ('req', 'tp'), axis=0, tiled=True)  46.7 us
    all_gather x1, blocking collectives, local(): lax.all_gather(k_cast, ('req', 'tp'), axis=0, tiled=True)  37.9 us
    dot_general x1, matrix products, local(): jnp.dot(hidden_ff, down_weight, preferred_element_type=jnp.float32)  11.4 us
  transfers between devices with their start and end apart: 7, of which 6 were waited for; matrix products, arithmetic and copies ran while one was open for 12% of the time, Pallas kernels for 0%

commit v1 on v0

--- a/solution.py
+++ b/solution.py
@@ -51,30 +51,44 @@
     down_master,
 ):
     tp_count = lax.axis_size("tp")
+    req_count = lax.axis_size("req")
     tensor_shard_index = lax.axis_index("tp")
-    q_cast = q_master.astype(jnp.bfloat16)
-    k_cast = k_master.astype(jnp.bfloat16)
-    v_cast = trainer_value_weight.astype(jnp.bfloat16)
-    o_cast = o_master.astype(jnp.bfloat16)
-    gate_cast = gate_master.astype(jnp.bfloat16)
-    up_cast = up_master.astype(jnp.bfloat16)
-    down_cast = down_master.astype(jnp.bfloat16)
+    half = jnp.bfloat16
+    shard_rows = q_master.shape[0]
     q_cols = q_master.shape[1] // tp_count
+    kv_cols = k_master.shape[1]
     ff_cols = gate_master.shape[1] // tp_count
-    q_full, key_weight, value_weight, o_full, gate_full, up_full, down_full = (
-        lax.all_gather(q_cast, ("req", "tp"), axis=0, tiled=True),
-        lax.all_gather(k_cast, ("req", "tp"), axis=0, tiled=True),
-        lax.all_gather(v_cast, ("req", "tp"), axis=0, tiled=True),
-        lax.all_gather(o_cast, ("req", "tp"), axis=0, tiled=True),
-        lax.all_gather(gate_cast, ("req", "tp"), axis=0, tiled=True),
-        lax.all_gather(up_cast, ("req", "tp"), axis=0, tiled=True),
-        lax.all_gather(down_cast, ("req", "tp"), axis=0, tiled=True),
+    down_rows = down_master.shape[0]
+
+    q_parts = q_master.reshape(shard_rows, tp_count, q_cols).transpose(1, 0, 2)
+    kv_parts = jnp.broadcast_to(
+        jnp.concatenate([k_master, trainer_value_weight], axis=1)[None],
+        (tp_count, shard_rows, 2 * kv_cols),
     )
-    query_weight = lax.dynamic_slice_in_dim(q_full, tensor_shard_index * q_cols, q_cols, 1)
-    gate_weight = lax.dynamic_slice_in_dim(gate_full, tensor_shard_index * ff_cols, ff_cols, 1)
-    up_weight = lax.dynamic_slice_in_dim(up_full, tensor_shard_index * ff_cols, ff_cols, 1)
-    out_weight = lax.dynamic_slice_in_dim(o_full, tensor_shard_index * q_cols, q_cols, 0)
-    down_weight = lax.dynamic_slice_in_dim(down_full, tensor_shard_index * ff_cols, ff_cols, 0)
+    first_pack = jnp.concatenate([q_parts, kv_parts], axis=2).astype(half)
+    first_pack = first_pack.reshape(tp_count * shard_rows, q_cols + 2 * kv_cols)
+    first_pack = lax.all_to_all(first_pack, "tp", 0, 0, tiled=True)
+    first_full = lax.all_gather(first_pack, "req", axis=0, tiled=True)
+
+    def ff_parts(master):
+        return (
+            master.astype(half)
+            .reshape(shard_rows, req_count, tp_count, down_rows)
+            .transpose(2, 0, 1, 3)
+            .reshape(tp_count * shard_rows, ff_cols)
+        )
+
+    second_pack = jnp.concatenate([ff_parts(gate_master), ff_parts(up_master)], axis=1)
+    second_pack = lax.all_to_all(second_pack, "tp", 0, 0, tiled=True)
+    o_full = lax.all_gather(o_master.astype(half), ("req", "tp"), axis=0, tiled=True)
+    second_full = lax.all_gather(second_pack, "req", axis=0, tiled=True)
+    down_weight = lax.all_gather(down_master.astype(half), "req", axis=0, tiled=True)
+
+    query_weight = first_full[:, :q_cols]
+    key_weight = first_full[:, q_cols : q_cols + kv_cols]
+    value_weight = first_full[:, q_cols + kv_cols :]
+    gate_weight = second_full[:, :ff_cols]
+    up_weight = second_full[:, ff_cols:]
     prompt_batch, sequence_length, model_width = hidden_in.shape
     tok_rows = prompt_batch * sequence_length
     flat_rows = hidden_in.reshape(tok_rows, model_width).astype(jnp.float32)
@@ -129,19 +143,21 @@
         .astype(jnp.bfloat16)
         .reshape(tok_rows, local_heads * HEAD_DIM)
     )
-    attn_total = lax.psum(
-        jnp.dot(attended, out_weight, preferred_element_type=jnp.float32).astype(jnp.bfloat16), "tp"
-    ).astype(jnp.float32)
-    middle = flat_rows + attn_total
-    normed_rows = rms_norm(middle, mlp_gain)
+    own_rows = tok_rows // tp_count
+    attended_rows = lax.all_to_all(attended, "tp", 0, 1, tiled=True)
+    own_hidden = lax.dynamic_slice_in_dim(flat_rows, tensor_shard_index * own_rows, own_rows, 0)
+    middle = own_hidden + jnp.dot(attended_rows, o_full, preferred_element_type=jnp.float32)
+    normed_rows = lax.all_gather(rms_norm(middle, mlp_gain), "tp", axis=0, tiled=True)
     gate_val = jnp.dot(normed_rows, gate_weight, preferred_element_type=jnp.float32)
     up_val = jnp.dot(normed_rows, up_weight, preferred_element_type=jnp.float32)
     hidden_ff = (jax.nn.silu(gate_val) * up_val).astype(jnp.bfloat16)
-    ffn_total = lax.psum(
+    ffn_rows = lax.psum_scatter(
         jnp.dot(hidden_ff, down_weight, preferred_element_type=jnp.float32).astype(jnp.bfloat16),
         "tp",
+        scatter_dimension=0,
+        tiled=True,
     ).astype(jnp.float32)
-    result = (middle + ffn_total).astype(jnp.bfloat16)
+    result = lax.all_gather((middle + ffn_rows).astype(jnp.bfloat16), "tp", axis=0, tiled=True)
     return (result.reshape(prompt_batch, sequence_length, model_width), kv_cache)
 
 

time: 534 us -> 382 us (0.72)
  waiting for transfers between devices: 346 us -> 257 us
  blocking collectives: 84.6 us -> 8.45 us
  local copies, waits for them, and re-layouts: 13.6 us -> 26.2 us
  starting transfers between devices: 0.51 us -> 12.2 us
  other arithmetic: 26 us -> 16.3 us
    psum x2 -> x0, waiting for transfers between devices: 108 us -> none  [the longest x1 56.1 us: local(): lax.psum(jnp.dot(attended, out_weight, preferred_element_type=jnp.float32...]
    all_gather x2 -> x0, blocking collectives: 84.6 us -> none  [the longest x1 46.7 us: local(): lax.all_gather(v_cast, ('req', 'tp'), axis=0, tiled=True)]
    reduce_scatter x0 -> x1, waiting for transfers between devices: none -> 33.4 us  [local(): lax.psum_scatter(jnp.dot(hidden_ff, down_weight, preferred_element_type=j...]
    all_gather x5 -> x6, waiting for transfers between devices: 238 us -> 208 us  [the longest x1 73 us: local(): second_full = lax.all_gather(second_pack, 'req', axis=0, tiled=True)]
    all_to_all x0 -> x2, waiting for transfers between devices: none -> 15 us  [the longest x1 7.57 us: local(): second_pack = lax.all_to_all(second_pack, 'tp', 0, 0, tiled=True)]
    all_to_all x0 -> x2, starting transfers between devices: none -> 12 us  [the longest x1 6.37 us: local(): attended_rows = lax.all_to_all(attended, 'tp', 0, 1, tiled=True)]
    all_to_all x0 -> x1, blocking collectives: none -> 8.45 us  [local(): first_pack = lax.all_to_all(first_pack, 'tp', 0, 0, tiled=True)]
    convert_element_type x8 -> x6, other arithmetic: 14.5 us -> 6.21 us  [the longest x1 2.72 us: local(): flat_rows = hidden_in.reshape(tok_rows, model_width).astype(jnp.float32)]
  transfers between devices with their start and end apart: 7 -> 9, of which waited for: 6 -> 9; matrix products, arithmetic and copies ran while one was open for 12% -> 16% of each run, Pallas kernels for 0% -> 0%
where the time goes in v1:
time: 382 us; the launch traced here: 379 us
  waiting for transfers between devices  257 us (67%)
  matrix products  44.7 us (12%)
  local copies, waits for them, and re-layouts  26.2 us (7%)
  other arithmetic  16.3 us (4%)
  between operations  14.4 us (4%)
  starting transfers between devices  12.2 us (3%)
  blocking collectives  8.45 us (2%)
    all_gather x1, waiting for transfers between devices, local(): second_full = lax.all_gather(second_pack, 'req', axis=0, tiled=True)  73 us
    all_gather x1, waiting for transfers between devices, local(): lax.all_gather(down_master.astype(half), 'req', axis=0, tiled=True)  46.4 us
    all_gather x1, waiting for transfers between devices, local(): first_full = lax.all_gather(first_pack, 'req', axis=0, tiled=True)  33.9 us
    reduce_scatter x1, waiting for transfers between devices, local(): lax.psum_scatter(jnp.dot(hidden_ff, down_weight, preferred_element_type=j...  33.4 us
    all_gather x1, waiting for transfers between devices, local(): lax.all_gather(rms_norm(middle, mlp_gain), 'tp', axis=0, tiled=True)  27.2 us
    all_gather x1, waiting for transfers between devices, local(): lax.all_gather((middle + ffn_rows).astype(jnp.bfloat16), 'tp', axis=0, ti...  23.9 us
    dot_general x1, matrix products, local(): jnp.dot(hidden_ff, down_weight, preferred_element_type=jnp.float32)  11.4 us
    sub x1, matrix products, local(): expo = jnp.exp(scores - highest)  9.63 us
  transfers between devices with their start and end apart: 9, of which 9 were waited for; matrix products, arithmetic and copies ran while one was open for 16% of the time, Pallas kernels for 0%

profile of v1, /device:TPU:13, one launch (start us, length us, event | category | flops | bytes accessed | tf_op | source)
XLA Modules:
  0.0 379.1 jit_solution(6430211192433051770)
XLA Ops:
  7.2 0.0 all-gather.7.cloned.1.call-start
  7.2 1.0 convert.16
  8.2 0.2 reshape.212
  8.5 1.0 maximum_convert_fusion.1
  9.5 0.1 pad_maximum_fusion.9
  9.6 8.5 %all_to_all.37 = bf16[4,40,960]{2,1,0:T(8,128)(2,1)} all-to-all(bf16[4,40,960]{2,1,0:T(8,128)(2,1)S(1)} %pad_maximum_fusion.9), channel_id=1, replica_groups=mesh['req'=8,'tp'=4] {'tp'}, dimensions={0} | all-to-all | bytes 614400 | tf_op jit(solution)/shard_map/all_to_all | solution.py:70
  18.1 0.0 all-gather.7.cloned.1.call-update
  18.1 0.0 all-gather.9.cloned.1.call-start
  18.2 0.7 convert_element_type.94
  18.8 0.0 all-gather.9.cloned.1.call-update
  18.9 0.4 reshape.213
  19.4 1.0 concatenate.31
  20.5 0.4 reshape.214
  21.0 0.3 concatenate.32
  21.2 1.8 pad_maximum_fusion.2
  23.1 5.6 %all-to-all-start.2 = ((bf16[4,40,1792]{2,1,0:T(8,128)(2,1)}), bf16[4,40,1792]{2,1,0:T(8,128)(2,1)S(1)}, u32[]{:S(2)}, u32[]{:S(2)}) async-start(bf16[4,40,1792]{2,1,0:T(8,128)(2,1)} %pad_maximum_fusion.2), calls=%async_computation.2 | async-start | bytes 1146880 | tf_op jit(solution)/shard_map/all_to_all | solution.py:82
  28.7 7.6 %all-to-all-done.2 = bf16[4,40,1792]{2,1,0:T(8,128)(2,1)S(1)} async-done(((bf16[4,40,1792]{2,1,0:T(8,128)(2,1)}), bf16[4,40,1792]{2,1,0:T(8,128)(2,1)S(1)}, u32[]{:S(2)}, u32[]{:S(2)}) %all-to-all-start.2) | async-done | bytes 573472 | tf_op jit(solution)/shard_map/all_to_all | solution.py:82
  36.3 0.8 copy-done.3
  37.1 0.1 iota_compare_fusion
  37.2 0.1 iota_compare_fusion.1
  37.3 0.6 multiply_reduce_fusion
  37.9 0.3 fusion.36
  38.2 1.1 broadcast_and_fusion
  39.4 33.9 %all-gather.7.cloned.1.call-done = bf16[1280,960]{1,0:T(8,128)(2,1)} async-done(((bf16[160,960]{1,0:T(8,128)(2,1)}), bf16[1280,960]{1,0:T(8,128)(2,1)}) %all-gather.7.cloned.1.call-update) | async-done | bytes 2457616 | tf_op jit(solution)/shard_map/all_gather | solution.py:71
  73.3 4.0 %slice_bitcast_fusion.2 = (bf16[320,1280]{0,1:T(8,128)(2,1)}, bf16[320,1280]{0,1:T(8,128)(2,1)}, bf16[320,1280]{0,1:T(8,128)(2,1)}) fusion(bf16[1280,960]{1,0:T(8,128)(2,1)} %all-gather.7.cloned.1.call-done), kind=kLoop, calls=%fused_computation.39 | loop fusion | bytes 4915200 | tf_op jit(solution)/shard_map/dot_general | solution.py:103
  77.2 2.3 copy.47
  79.5 2.2 copy.46
  81.7 2.2 copy.44
  83.9 2.3 fusion.30
  86.2 0.2 multiply_subtract_fusion
  86.5 0.9 copy-done.5
  87.3 1.1 fusion.32
  88.5 1.1 subtract_convert_fusion
  89.6 1.5 fusion.17
  91.1 1.2 convolution_convert_fusion.3
  92.3 0.8 copy-done.1
  93.1 1.5 fusion.16
  94.6 9.6 %fusion.49 = (f32[2,5,512]{2,1,0:T(8,128)S(1)}, f32[2,5,512,512]{2,3,1,0:T(8,128)}) fusion(pred[2,512,512]{1,2,0:T(8,128)(4,1)} %broadcast_and_fusion, bf16[2,512,5,32]{1,3,2,0:T(8,128)(2,1)} %get-tuple-element.8, bf16[2,512,5,32]{1,3,2,0:T(8,128)(2,1)} %get-tuple-element.7, bf16[2,512,5,64]{1,2,3,0:T(8,128)(2,1)} %fusion.17), kind=kOutput, calls=%fused_computation.76 | convolution fusion | flops 347341312 | bytes 12341248 | tf_op jit(solution)/shard_map/sub | solution.py:139
  104.3 5.4 %fusion.19 = bf16[2,512,5,64]{1,3,2,0:T(8,128)(2,1)S(1)} fusion(f32[2,5,512,512]{2,3,1,0:T(8,128)} %get-tuple-element.12, f32[2,5,512]{2,1,0:T(8,128)S(1)} %get-tuple-element.11, bf16[2,512,5,64]{1,2,3,0:T(8,128)(2,1)} %fusion.16), kind=kOutput, calls=%fused_computation.31 | convolution fusion | flops 341114880 | bytes 11816960 | tf_op jit(solution)/shard_map/phqk,pkhd->pqhd/dot_general | solution.py:142
  109.6 1.5 copy.52
  111.1 3.0 all_to_all.28
  114.2 2.0 copy.53
  116.2 6.4 %all-to-all-start.1 = ((bf16[4,256,320]{1,2,0:T(8,128)(2,1)}), bf16[4,256,320]{1,2,0:T(8,128)(2,1)}, u32[]{:S(2)}, u32[]{:S(2)}) async-start(bf16[4,256,320]{1,2,0:T(8,128)(2,1)} %copy.53), calls=%async_computation.1 | async-start | bytes 1310720 | tf_op jit(solution)/shard_map/all_to_all | solution.py:147
  122.5 2.7 convert.23
  125.3 7.4 %all-to-all-done.1 = bf16[4,256,320]{1,2,0:T(8,128)(2,1)} async-done(((bf16[4,256,320]{1,2,0:T(8,128)(2,1)}), bf16[4,256,320]{1,2,0:T(8,128)(2,1)}, u32[]{:S(2)}, u32[]{:S(2)}) %all-to-all-start.1) | async-done | bytes 655392 | tf_op jit(solution)/shard_map/all_to_all | solution.py:147
  132.6 3.9 %all-gather.9.cloned.1.call-done = bf16[1280,1280]{1,0:T(8,128)(2,1)} async-done(((bf16[40,1280]{1,0:T(8,128)(2,1)}), bf16[1280,1280]{1,0:T(8,128)(2,1)}) %all-gather.9.cloned.1.call-update) | async-done | bytes 3276816 | tf_op jit(solution)/shard_map/all_gather | solution.py:83
  136.6 3.6 multiply_reduce_fusion.1
  140.2 1.0 multiply_convert_fusion.3
  141.3 0.0 all-gather.15.cloned.1.call-start
  141.3 0.7 convert_element_type.99
  142.1 0.0 reduce-scatter.2.cloned.1.call-start
  142.2 73.0 %all-gather.13.cloned.1.call-done = bf16[1280,1792]{1,0:T(8,128)(2,1)} async-done(((bf16[160,1792]{1,0:T(8,128)(2,1)}), bf16[1280,1792]{1,0:T(8,128)(2,1)}) %all-gather.13.cloned.1.call-update) | async-done | bytes 4587536 | tf_op jit(solution)/shard_map/all_gather | solution.py:84
  215.2 27.2 %all-gather.11.cloned.1.call-done = bf16[1024,1280]{1,0:T(8,128)(2,1)} async-done(((bf16[256,1280]{1,0:T(8,128)(2,1)}), bf16[1024,1280]{1,0:T(8,128)(2,1)}) %all-gather.11.cloned.1.call-update) | async-done | bytes 2621456 | tf_op jit(solution)/shard_map/all_gather | solution.py:150
  242.3 7.1 %fusion.7 = f32[1024,896]{1,0:T(8,128)} fusion(bf16[1024,1280]{1,0:T(8,128)(2,1)} %all-gather.11.cloned.1.call-done, bf16[1280,1792]{1,0:T(8,128)(2,1)} %all-gather.13.cloned.1.call-done), kind=kOutput, calls=%fused_computation.15 | convolution fusion | flops 2348810240 | bytes 8585216 | tf_op jit(solution)/shard_map/dot_general | solution.py:152
  249.4 46.4 %all-gather.15.cloned.1.call-done = bf16[896,1280]{1,0:T(8,128)(2,1)} async-done(((bf16[112,1280]{1,0:T(8,128)(2,1)}), bf16[896,1280]{1,0:T(8,128)(2,1)}) %all-gather.15.cloned.1.call-update) | async-done | bytes 2293776 | tf_op jit(solution)/shard_map/all_gather | solution.py:85
  295.8 11.4 %convolution_convert_fusion = bf16[1024,1280]{1,0:T(8,128)(2,1)} fusion(bf16[896,1280]{1,0:T(8,128)(2,1)} %all-gather.15.cloned.1.call-done, f32[1024,896]{1,0:T(8,128)} %fusion.7, bf16[1024,1280]{1,0:T(8,128)(2,1)} %all-gather.11.cloned.1.call-done, bf16[1280,1792]{1,0:T(8,128)(2,1)} %all-gather.13.cloned.1.call-done), kind=kOutput, calls=%fused_computation.11 | convolution fusion | flops 4704436224 | bytes 13500416 | tf_op jit(solution)/shard_map/dot_general | solution.py:155
  307.2 0.0 all-gather.17.cloned.1.call-start
  307.2 33.4 %reduce-scatter.2.cloned.1.call-done = bf16[256,1280]{1,0:T(8,128)(2,1)} async-done(((bf16[1024,1280]{1,0:T(8,128)(2,1)}), bf16[256,1280]{1,0:T(8,128)(2,1)}) %reduce-scatter.2.cloned.1.call-update) | async-done | bytes 655376 | tf_op jit(solution)/shard_map/reduce_scatter | solution.py:154
  340.6 2.0 add_convert_fusion
  342.7 0.4 copy.56
  343.1 0.4 copy.57
  343.4 1.5 pad_maximum_fusion
  344.9 23.9 %all-gather.17.cloned.1.call-done = bf16[1024,1280]{1,0:T(8,128)(2,1)} async-done(((bf16[256,1280]{1,0:T(8,128)(2,1)}), bf16[1024,1280]{1,0:T(8,128)(2,1)}) %all-gather.17.cloned.1.call-update) | async-done | bytes 2621456 | tf_op jit(solution)/shard_map/all_gather | solution.py:160
  368.9 3.4 copy.82
  (41 shorter events, 0.4 us)
Async XLA Ops:
  7.2 11.0 %copy-start.9 = (f32[40,1280]{1,0:T(8,128)S(1)}, f32[40,1280]{1,0:T(8,128)}, u32[]{:S(2)}) copy-start(f32[40,1280]{1,0:T(8,128)} %param.18) | copy-start | bytes 614404
  7.2 11.7 %copy-start.6 = (f32[40,3584]{1,0:T(8,128)S(1)}, f32[40,3584]{1,0:T(8,128)}, u32[]{:S(2)}) copy-start(f32[40,3584]{1,0:T(8,128)} %param.19) | copy-start | bytes 1720324
  7.2 66.1 %all-gather.7.cloned.1.call-start = ((), (), s32[]{:S(2)}) async-start(), calls=%async_computation.4 | async-start | bytes 2949120 | tf_op jit(solution)/shard_map/all_gather | solution.py:71
  8.4 12.0 %copy-start.7 = (f32[40,3584]{1,0:T(8,128)S(1)}, f32[40,3584]{1,0:T(8,128)}, u32[]{:S(2)}) copy-start(f32[40,3584]{1,0:T(8,128)} %param.20) | copy-start | bytes 1720324
  18.1 118.5 %all-gather.9.cloned.1.call-start = ((), (), s32[]{:S(2)}) async-start(), calls=%async_computation.5 | async-start | bytes 3379200 | tf_op jit(solution)/shard_map/all_gather | solution.py:83
  20.4 16.8 %copy-start.11 = (s32[2]{0:T(128)S(1)}, s32[2]{0:T(128)}, u32[]{:S(2)}) copy-start(s32[2]{0:T(128)} %param.12) | copy-start | bytes 28
  20.4 16.9 %copy-start = (bf16[2,512,1280]{2,1,0:T(8,128)(2,1)S(1)}, bf16[2,512,1280]{2,1,0:T(8,128)(2,1)}, u32[]{:S(2)}) copy-start(bf16[2,512,1280]{2,1,0:T(8,128)(2,1)} %param.11) | copy-start | bytes 7864324
  23.1 13.2 %all-to-all-start.2 = ((bf16[4,40,1792]{2,1,0:T(8,128)(2,1)}), bf16[4,40,1792]{2,1,0:T(8,128)(2,1)S(1)}, u32[]{:S(2)}, u32[]{:S(2)}) async-start(bf16[4,40,1792]{2,1,0:T(8,128)(2,1)} %pad_maximum_fusion.2), calls=%async_computation.2 | async-start | bytes 1146880 | tf_op jit(solution)/shard_map/all_to_all | solution.py:82
  28.7 186.5 %all-gather.13.cloned.1.call-start = ((), (), s32[]{:S(2)}) async-start(), calls=%async_computation.7 | async-start | bytes 5160960 | tf_op jit(solution)/shard_map/all_gather | solution.py:84
  36.3 0.8 copy-start.3
  77.2 6.6 %copy-start.12 = (f32[1280]{0:T(1024)S(1)}, f32[1280]{0:T(1024)}, u32[]{:S(2)}) copy-start(f32[1280]{0:T(1024)} %param.13) | copy-start | bytes 15364
  86.2 1.1 copy-start.5
  88.5 2.6 copy-start.4
  92.3 0.8 copy-start.1
  116.2 16.5 %all-to-all-start.1 = ((bf16[4,256,320]{1,2,0:T(8,128)(2,1)}), bf16[4,256,320]{1,2,0:T(8,128)(2,1)}, u32[]{:S(2)}, u32[]{:S(2)}) async-start(bf16[4,256,320]{1,2,0:T(8,128)(2,1)} %copy.53), calls=%async_computation.1 | async-start | bytes 1310720 | tf_op jit(solution)/shard_map/all_to_all | solution.py:147
  122.5 119.8 %all-gather.11.cloned.1.call-start = ((), (), s32[]{:S(2)}) async-start(), calls=%async_computation.6 | async-start | bytes 3276800 | tf_op jit(solution)/shard_map/all_gather | solution.py:150
  136.6 3.7 copy-start.10
  140.2 1.1 copy-start.8
  141.3 154.5 %all-gather.15.cloned.1.call-start = ((), (), s32[]{:S(2)}) async-start(), calls=%async_computation.8 | async-start | bytes 2580480 | tf_op jit(solution)/shard_map/all_gather | solution.py:85
  142.1 198.5 %reduce-scatter.2.cloned.1.call-start = ((), (), s32[]{:S(2)}) async-start(), calls=%async_computation.9 | async-start | bytes 3276800 | tf_op jit(solution)/shard_map/reduce_scatter | solution.py:154
  307.2 35.9 %copy-start.2 = (bf16[2,512,5,64]{1,3,2,0:T(8,128)(2,1)S(1)}, bf16[2,512,5,64]{1,3,2,0:T(8,128)(2,1)}, u32[]{:S(2)}) copy-start(bf16[2,512,5,64]{1,3,2,0:T(8,128)(2,1)} %copy-done.1) | copy-start | bytes 1966084
  307.2 61.7 %all-gather.17.cloned.1.call-start = ((), (), s32[]{:S(2)}) async-start(), calls=%async_computation.10 | async-start | bytes 3276800 | tf_op jit(solution)/shard_map/all_gather | solution.py:160
Sparse Core Ops, SparseCore 0:
  18.2 55.0 all-gather.6
  76.1 60.4 all-gather.8
  138.8 76.3 all-gather.12
  217.2 25.1 all-gather.10
  244.9 50.7 all-gather.14
  307.3 33.2 reduce-scatter.1
  342.9 25.9 all-gather.16

commit v2 on v1

--- a/solution.py
+++ b/solution.py
@@ -35,6 +35,53 @@
         [first_half * cos_b - second_half * sin_b, second_half * cos_b + first_half * sin_b],
         axis=-1,
     )
+
+
+def tp_permute(field, flip):
+    return lax.ppermute(field, "tp", [(s, s ^ flip) for s in range(lax.axis_size("tp"))])
+
+
+def gather_req(shard):
+    count = lax.axis_size("req")
+    inner = 2
+    outer = count // inner
+    me = lax.axis_index("req")
+    far, near = me // inner, me % inner
+    out = jnp.zeros((outer, inner) + shard.shape, shard.dtype)
+    zeros = (0,) * shard.ndim
+    for step in range(outer):
+        held = shard
+        if step:
+            pairs = [(r, (r + step * inner) % count) for r in range(count)]
+            held = lax.ppermute(shard, "req", pairs)
+        other = lax.ppermute(held, "req", [(r, r ^ 1) for r in range(count)])
+        place = (far + outer - step) % outer
+        out = lax.dynamic_update_slice(out, held[None, None], (place, near) + zeros)
+        out = lax.dynamic_update_slice(out, other[None, None], (place, 1 - near) + zeros)
+    return out.reshape((count,) + shard.shape)
+
+
+def gather_tp(rows):
+    me = lax.axis_index("tp")
+    high, low = me // 2, me % 2
+    across = tp_permute(rows, 2)
+    pair = jnp.where(high == 0, jnp.stack([rows, across]), jnp.stack([across, rows]))
+    twin = tp_permute(pair, 1)
+    whole = jnp.where(low == 0, jnp.stack([pair, twin], 1), jnp.stack([twin, pair], 1))
+    return whole.reshape((4,) + rows.shape)
+
+
+def scatter_tp(parts):
+    me = lax.axis_index("tp")
+    high, low = me // 2, me % 2
+    rows, width = parts.shape
+    parts = parts.reshape(2, 2, rows // 4, width)
+    twin = tp_permute(lax.dynamic_index_in_dim(parts, 1 - low, 1, keepdims=False), 1)
+    kept = lax.dynamic_index_in_dim(parts, low, 1, keepdims=False).astype(jnp.float32)
+    pair = kept + twin.astype(jnp.float32)
+    away = lax.dynamic_index_in_dim(pair, 1 - high, 0, keepdims=False).astype(jnp.bfloat16)
+    stay = lax.dynamic_index_in_dim(pair, high, 0, keepdims=False)
+    return stay + tp_permute(away, 2).astype(jnp.float32)
 
 
 def local(
@@ -68,7 +115,7 @@
     first_pack = jnp.concatenate([q_parts, kv_parts], axis=2).astype(half)
     first_pack = first_pack.reshape(tp_count * shard_rows, q_cols + 2 * kv_cols)
     first_pack = lax.all_to_all(first_pack, "tp", 0, 0, tiled=True)
-    first_full = lax.all_gather(first_pack, "req", axis=0, tiled=True)
+    first_full = gather_req(first_pack).reshape(-1, q_cols + 2 * kv_cols)
 
     def ff_parts(master):
         return (
@@ -80,9 +127,12 @@
 
     second_pack = jnp.concatenate([ff_parts(gate_master), ff_parts(up_master)], axis=1)
     second_pack = lax.all_to_all(second_pack, "tp", 0, 0, tiled=True)
-    o_full = lax.all_gather(o_master.astype(half), ("req", "tp"), axis=0, tiled=True)
-    second_full = lax.all_gather(second_pack, "req", axis=0, tiled=True)
-    down_weight = lax.all_gather(down_master.astype(half), "req", axis=0, tiled=True)
+    first_full, second_pack, o_own, down_own = lax.optimization_barrier(
+        (first_full, second_pack, o_master.astype(half), down_master.astype(half))
+    )
+    o_full = gather_tp(gather_req(o_own)).transpose(1, 0, 2, 3).reshape(-1, o_own.shape[1])
+    second_full = gather_req(second_pack).reshape(-1, 2 * ff_cols)
+    down_weight = gather_req(down_own).reshape(ff_cols, down_own.shape[1])
 
     query_weight = first_full[:, :q_cols]
     key_weight = first_full[:, q_cols : q_cols + kv_cols]
@@ -147,17 +197,14 @@
     attended_rows = lax.all_to_all(attended, "tp", 0, 1, tiled=True)
     own_hidden = lax.dynamic_slice_in_dim(flat_rows, tensor_shard_index * own_rows, own_rows, 0)
     middle = own_hidden + jnp.dot(attended_rows, o_full, preferred_element_type=jnp.float32)
-    normed_rows = lax.all_gather(rms_norm(middle, mlp_gain), "tp", axis=0, tiled=True)
+    normed_rows = gather_tp(rms_norm(middle, mlp_gain)).reshape(tok_rows, model_width)
     gate_val = jnp.dot(normed_rows, gate_weight, preferred_element_type=jnp.float32)
     up_val = jnp.dot(normed_rows, up_weight, preferred_element_type=jnp.float32)
     hidden_ff = (jax.nn.silu(gate_val) * up_val).astype(jnp.bfloat16)
-    ffn_rows = lax.psum_scatter(
-        jnp.dot(hidden_ff, down_weight, preferred_element_type=jnp.float32).astype(jnp.bfloat16),
-        "tp",
-        scatter_dimension=0,
-        tiled=True,
-    ).astype(jnp.float32)
-    result = lax.all_gather((middle + ffn_rows).astype(jnp.bfloat16), "tp", axis=0, tiled=True)
+    ffn_rows = scatter_tp(
+        jnp.dot(hidden_ff, down_weight, preferred_element_type=jnp.float32).astype(jnp.bfloat16)
+    )
+    result = gather_tp((middle + ffn_rows).astype(jnp.bfloat16))
     return (result.reshape(prompt_batch, sequence_length, model_width), kv_cache)
 
 

time: 382 us -> 339 us (0.89)
  waiting for transfers between devices: 257 us -> 179 us
  starting transfers between devices: 12.2 us -> 42.9 us
  other arithmetic: 16.3 us -> 30.3 us
  local copies, waits for them, and re-layouts: 26.2 us -> 39.9 us
  between operations: 14.4 us -> 1.46 us
  blocking collectives: 8.45 us -> 0 us
    all_gather x6 -> x0, waiting for transfers between devices: 208 us -> none  [the longest x1 73 us: local(): second_full = lax.all_gather(second_pack, 'req', axis=0, tiled=True)]
    ppermute x0 -> x36, waiting for transfers between devices: none -> 179 us  [the longest x12 71.4 us: gather_req(): held = lax.ppermute(shard, 'req', pairs)]
    reduce_scatter x1 -> x0, waiting for transfers between devices: 33.4 us -> none  [local(): lax.psum_scatter(jnp.dot(hidden_ff, down_weight, preferred_element_type=j...]
    ppermute x0 -> x36, starting transfers between devices: none -> 27.8 us  [the longest x12 12.1 us: gather_req(): held = lax.ppermute(shard, 'req', pairs)]
    dynamic_update_slice x0 -> x32, local copies, waits for them, and re-layouts: none -> 10.8 us  [the longest x16 5.68 us: gather_req(): out = lax.dynamic_update_slice(out, held[None, None], (place, near) + zeros)]
    all_to_all x1 -> x0, blocking collectives: 8.45 us -> none  [local(): first_pack = lax.all_to_all(first_pack, 'tp', 0, 0, tiled=True)]
    all_to_all x1, waiting for transfers between devices: 7.57 us -> 0.01 us  [local(): second_pack = lax.all_to_all(second_pack, 'tp', 0, 0, tiled=True)]
    all_to_all x1, waiting for transfers between devices: 7.39 us -> 0.01 us  [local(): attended_rows = lax.all_to_all(attended, 'tp', 0, 1, tiled=True)]
  transfers between devices with their start and end apart: 9 -> 39, of which waited for: 9 -> 19; matrix products, arithmetic and copies ran while one was open for 16% -> 23% of each run, Pallas kernels for 0% -> 0%
where the time goes in v2:
time: 339 us; the launch traced here: 337 us
  waiting for transfers between devices  179 us (53%)
  matrix products  43.9 us (13%)
  starting transfers between devices  42.9 us (13%)
  local copies, waits for them, and re-layouts  39.9 us (12%)
  other arithmetic  30.3 us (9%)
    ppermute x12, waiting for transfers between devices, gather_req(): held = lax.ppermute(shard, 'req', pairs)  71.4 us
    ppermute x8, waiting for transfers between devices, tp_permute(): lax.ppermute(field, 'tp', [(s, s ^ flip) for s in range(lax.axis_size('tp...  64.6 us
    ppermute x16, waiting for transfers between devices, gather_req(): other = lax.ppermute(held, 'req', [(r, r ^ 1) for r in range(count)])  42.9 us
    ppermute x12, starting transfers between devices, gather_req(): held = lax.ppermute(shard, 'req', pairs)  12.1 us
    dot_general x1, matrix products, local(): jnp.dot(hidden_ff, down_weight, preferred_element_type=jnp.float32)  11.4 us
    ppermute x16, starting transfers between devices, gather_req(): other = lax.ppermute(held, 'req', [(r, r ^ 1) for r in range(count)])  9.79 us
    sub x1, matrix products, local(): expo = jnp.exp(scores - highest)  9.34 us
    all_to_all x1, starting transfers between devices, local(): attended_rows = lax.all_to_all(attended, 'tp', 0, 1, tiled=True)  7.34 us
  transfers between devices with their start and end apart: 39, of which 19 were waited for; matrix products, arithmetic and copies ran while one was open for 23% of the time, Pallas kernels for 0%

profile of v2, /device:TPU:13, one launch (start us, length us, event | category | flops | bytes accessed | tf_op | source)
XLA Modules:
  0.0 337.4 jit_solution(1195818114729728157)
XLA Ops:
  3.7 4.2 %all-to-all-start = ((bf16[4,40,960]{2,1,0:T(8,128)(2,1)}), bf16[4,40,960]{2,1,0:T(8,128)(2,1)S(1)}, u32[]{:S(2)}, u32[]{:S(2)}) async-start(bf16[4,40,960]{2,1,0:T(8,128)(2,1)} %pad_maximum_fusion.9), calls=%async_computation | async-start | bytes 655360 | tf_op jit(solution)/shard_map/all_to_all | solution.py:117
  9.6 1.5 reshape.414
  11.9 2.0 concatenate.72
  13.9 1.8 convert_element_type.100
  15.7 1.4 reshape.413
  17.8 1.3 concatenate.71
  19.8 2.1 broadcast_and_fusion
  22.7 1.6 convert_element_type.102
  24.3 1.8 convert_element_type.103
  26.1 2.7 convert.26
  29.8 3.5 %all-to-all-start.1 = ((bf16[4,40,1792]{2,1,0:T(8,128)(2,1)}), bf16[4,40,1792]{2,1,0:T(8,128)(2,1)S(1)}, u32[]{:S(2)}, u32[]{:S(2)}) async-start(bf16[4,40,1792]{2,1,0:T(8,128)(2,1)} %pad_maximum_fusion.2), calls=%async_computation.1 | async-start | bytes 1146880 | tf_op jit(solution)/shard_map/all_to_all | solution.py:129
  33.3 1.3 collective-permute-start
  34.5 1.3 collective-permute-start.1
  36.8 1.5 collective-permute-start.5
  38.7 4.5 %collective-permute-done.1 = bf16[160,960]{1,0:T(8,128)(2,1)S(1)} collective-permute-done((bf16[160,960]{1,0:T(8,128)(2,1)S(1)}, bf16[160,960]{1,0:T(8,128)(2,1)S(1)}, u32[]{:S(2)}, u32[]{:S(2)}) %collective-permute-start.1) | collective-permute-done | bytes 307232 | tf_op jit(solution)/shard_map/ppermute | solution.py:56
  43.4 19.9 %collective-permute-done.3 = bf16[160,960]{1,0:T(8,128)(2,1)S(1)} collective-permute-done((bf16[160,960]{1,0:T(8,128)(2,1)S(1)}, bf16[160,960]{1,0:T(8,128)(2,1)S(1)}, u32[]{:S(2)}, u32[]{:S(2)}) %collective-permute-start.3) | collective-permute-done | bytes 307232 | tf_op jit(solution)/shard_map/ppermute | solution.py:56
  63.6 2.6 collective-permute-done.5
  66.5 4.5 %collective-permute-done.4 = bf16[160,960]{1,0:T(8,128)(2,1)S(1)} collective-permute-done((bf16[160,960]{1,0:T(8,128)(2,1)S(1)}, bf16[160,960]{1,0:T(8,128)(2,1)S(1)}, u32[]{:S(2)}, u32[]{:S(2)}) %collective-permute-start.4) | collective-permute-done | bytes 307232 | tf_op jit(solution)/shard_map/ppermute | solution.py:57
  71.1 6.9 %collective-permute-done.6 = bf16[160,960]{1,0:T(8,128)(2,1)S(1)} collective-permute-done((bf16[160,960]{1,0:T(8,128)(2,1)S(1)}, bf16[160,960]{1,0:T(8,128)(2,1)S(1)}, u32[]{:S(2)}, u32[]{:S(2)}) %collective-permute-start.6) | collective-permute-done | bytes 307232 | tf_op jit(solution)/shard_map/ppermute | solution.py:57
  78.4 3.1 collective-permute-start.10
  81.5 1.5 collective-permute-start.12
  83.0 2.2 slice_bitcast_fusion.2
  85.1 1.7 copy.68
  86.8 2.2 copy.69
  89.0 1.9 fusion.36
  94.4 2.2 copy.66
  96.6 2.3 convolution_convert_fusion.3
  99.1 1.5 fusion.17
  101.2 9.3 %fusion.53 = (f32[2,5,512]{2,1,0:T(8,128)S(1)}, f32[2,5,512,512]{2,3,1,0:T(8,128)}) fusion(pred[2,512,512]{1,2,0:T(8,128)(4,1)S(1)} %copy-done.18, bf16[2,512,5,32]{1,3,2,0:T(8,128)(2,1)} %get-tuple-element.16, bf16[2,512,5,32]{1,3,2,0:T(8,128)(2,1)S(1)} %copy-done.20, bf16[2,512,5,64]{1,2,3,0:T(8,128)(2,1)} %fusion.17), kind=kOutput, calls=%fused_computation.125 | convolution fusion | flops 347341312 | bytes 12341248 | tf_op jit(solution)/shard_map/sub | solution.py:189
  110.5 5.0 %fusion.22 = bf16[2,512,5,64]{1,3,2,0:T(8,128)(2,1)S(1)} fusion(f32[2,5,512,512]{2,3,1,0:T(8,128)} %get-tuple-element.20, f32[2,5,512]{2,1,0:T(8,128)S(1)} %get-tuple-element.19, bf16[2,512,5,64]{1,2,3,0:T(8,128)(2,1)S(1)} %fusion.16), kind=kOutput, calls=%fused_computation.47 | convolution fusion | flops 341114880 | bytes 11816960 | tf_op jit(solution)/shard_map/phqk,pkhd->pqhd/dot_general | solution.py:192
  117.4 7.3 %all-to-all-start.2 = ((bf16[4,256,320]{1,2,0:T(8,128)(2,1)}), bf16[4,256,320]{1,2,0:T(8,128)(2,1)S(1)}, u32[]{:S(2)}, u32[]{:S(2)}) async-start(bf16[4,256,320]{1,2,0:T(8,128)(2,1)} %copy.75), calls=%async_computation.2 | async-start | bytes 1310720 | tf_op jit(solution)/shard_map/all_to_all | solution.py:197
  124.8 1.2 collective-permute-start.25
  129.6 1.8 collective-permute-start.28
  131.4 3.9 %collective-permute-done.9 = bf16[40,1280]{1,0:T(8,128)(2,1)S(1)} collective-permute-done((bf16[40,1280]{1,0:T(8,128)(2,1)}, bf16[40,1280]{1,0:T(8,128)(2,1)S(1)}, u32[]{:S(2)}, u32[]{:S(2)}) %collective-permute-start.9) | collective-permute-done | bytes 102432 | tf_op jit(solution)/shard_map/ppermute | solution.py:57
  137.7 1.5 collective-permute-done.11
  140.5 13.6 %collective-permute-done.13 = bf16[40,1280]{1,0:T(8,128)(2,1)S(1)} collective-permute-done((bf16[40,1280]{1,0:T(8,128)(2,1)S(1)}, bf16[40,1280]{1,0:T(8,128)(2,1)S(1)}, u32[]{:S(2)}, u32[]{:S(2)}) %collective-permute-start.13) | collective-permute-done | bytes 102432 | tf_op jit(solution)/shard_map/ppermute | solution.py:57
  154.1 1.8 collective-permute-start.21
  156.4 5.7 %collective-permute-done.27 = bf16[112,1280]{1,0:T(8,128)(2,1)S(1)} collective-permute-done((bf16[112,1280]{1,0:T(8,128)(2,1)S(1)}, bf16[112,1280]{1,0:T(8,128)(2,1)S(1)}, u32[]{:S(2)}, u32[]{:S(2)}) %collective-permute-start.27) | collective-permute-done | bytes 286752 | tf_op jit(solution)/shard_map/ppermute | solution.py:57
  162.1 5.8 %collective-permute-done.29 = bf16[112,1280]{1,0:T(8,128)(2,1)S(1)} collective-permute-done((bf16[112,1280]{1,0:T(8,128)(2,1)S(1)}, bf16[112,1280]{1,0:T(8,128)(2,1)S(1)}, u32[]{:S(2)}, u32[]{:S(2)}) %collective-permute-start.29) | collective-permute-done | bytes 286752 | tf_op jit(solution)/shard_map/ppermute | solution.py:57
  167.9 44.5 %collective-permute-done.30 = bf16[112,1280]{1,0:T(8,128)(2,1)S(1)} collective-permute-done((bf16[112,1280]{1,0:T(8,128)(2,1)S(1)}, bf16[112,1280]{1,0:T(8,128)(2,1)S(1)}, u32[]{:S(2)}, u32[]{:S(2)}) %collective-permute-start.30) | collective-permute-done | bytes 286752 | tf_op jit(solution)/shard_map/ppermute | solution.py:56
  215.6 16.2 %collective-permute-done.14 = bf16[8,40,1280]{2,1,0:T(8,128)(2,1)S(1)} collective-permute-done((bf16[8,40,1280]{2,1,0:T(8,128)(2,1)S(1)}, bf16[8,40,1280]{2,1,0:T(8,128)(2,1)S(1)}, u32[]{:S(2)}, u32[]{:S(2)}) %collective-permute-start.14) | collective-permute-done | bytes 819232 | tf_op jit(solution)/shard_map/ppermute | solution.py:41
  232.0 1.4 collective-permute-start.15
  233.8 1.5 bitcast_dynamic-update-slice_fusion.3
  238.1 2.0 copy.76
  240.0 3.4 %multiply_reduce_fusion.1 = (f32[256]{0:T(256)S(1)}, f32[256,1280]{1,0:T(8,128)S(1)}) fusion(bf16[256,1280]{0,1:T(8,128)(2,1)S(1)} %bitcast.202, bf16[1280,1280]{1,0:T(8,128)(2,1)} %bitcast.178, f32[1024,1280]{1,0:T(8,128)} %convert.26, s32[]{:T(128)S(6)} %select_n.269), kind=kOutput, calls=%fused_computation.46 | convolution fusion | flops 839843584 | bytes 6554628 | tf_op jit(solution)/shard_map/dot_general | solution.py:199
  244.8 1.9 bitcast_dynamic-update-slice_fusion.2
  246.9 12.0 %collective-permute-done.16 = bf16[256,1280]{1,0:T(8,128)(2,1)S(1)} collective-permute-done((bf16[256,1280]{1,0:T(8,128)(2,1)S(1)}, bf16[256,1280]{1,0:T(8,128)(2,1)S(1)}, u32[]{:S(2)}, u32[]{:S(2)}) %collective-permute-start.16) | collective-permute-done | bytes 655392 | tf_op jit(solution)/shard_map/ppermute | solution.py:41
  259.1 2.1 collective-permute-start.17
  261.2 1.9 bitcast_dynamic-update-slice_fusion.1
  263.1 1.9 bitcast_dynamic-update-slice_fusion
  266.1 7.3 %fusion.7 = f32[1024,896]{1,0:T(8,128)} fusion(bf16[1024,1280]{1,0:T(8,128)(2,1)S(1)} %bitcast.194, bf16[1280,1792]{1,0:T(8,128)(2,1)} %bitcast.188), kind=kOutput, calls=%fused_computation.19 | convolution fusion | flops 2348810240 | bytes 8585216 | tf_op jit(solution)/shard_map/dot_general | solution.py:202
  273.4 11.4 %convolution_convert_fusion = bf16[1024,1280]{1,0:T(8,128)(2,1)} fusion(bf16[896,1280]{1,0:T(8,128)(2,1)} %bitcast.203, f32[1024,896]{1,0:T(8,128)} %fusion.7, bf16[1024,1280]{1,0:T(8,128)(2,1)} %bitcast.195, bf16[1280,1792]{1,0:T(8,128)(2,1)} %bitcast.189), kind=kOutput, calls=%fused_computation.11 | convolution fusion | flops 4704436224 | bytes 13500416 | tf_op jit(solution)/shard_map/dot_general | solution.py:205
  284.8 2.5 dynamic-slice_bitcast_fusion
  287.2 3.4 collective-permute-done.32
  290.6 2.0 convert_add_fusion
  292.6 1.5 copy-done.2
  294.3 16.2 %collective-permute-done.33 = bf16[256,1280]{1,0:T(8,128)(2,1)} collective-permute-done((bf16[256,1280]{1,0:T(8,128)(2,1)S(1)}, bf16[256,1280]{1,0:T(8,128)(2,1)}, u32[]{:S(2)}, u32[]{:S(2)}) %collective-permute-start.33) | collective-permute-done | bytes 655392 | tf_op jit(solution)/shard_map/ppermute | solution.py:41
  310.5 1.7 fusion.21
  312.4 15.2 %collective-permute-done.34 = bf16[256,1280]{1,0:T(8,128)(2,1)S(1)} collective-permute-done((bf16[256,1280]{1,0:T(8,128)(2,1)S(1)}, bf16[256,1280]{1,0:T(8,128)(2,1)S(1)}, u32[]{:S(2)}, u32[]{:S(2)}) %collective-permute-start.34) | collective-permute-done | bytes 655392 | tf_op jit(solution)/shard_map/ppermute | solution.py:41
  327.6 1.3 maximum_select_fusion.7
  328.8 1.9 collective-permute-start.35
  331.4 1.5 pad_maximum_fusion
  333.7 2.0 maximum_select_fusion.2
  335.7 1.7 copy.81
  (169 shorter events, 35.9 us)
Async XLA Ops:
  0.6 8.1 %copy-start.22 = (s32[2]{0:T(128)S(1)}, s32[2]{0:T(128)}, u32[]{:S(2)}) copy-start(s32[2]{0:T(128)} %param.12) | copy-start | bytes 28
  0.6 8.2 %copy-start.17 = (f32[40,3584]{1,0:T(8,128)S(1)}, f32[40,3584]{1,0:T(8,128)}, u32[]{:S(2)}) copy-start(f32[40,3584]{1,0:T(8,128)} %param.20) | copy-start | bytes 1720324
  3.7 26.1 %all-to-all-start = ((bf16[4,40,960]{2,1,0:T(8,128)(2,1)}), bf16[4,40,960]{2,1,0:T(8,128)(2,1)S(1)}, u32[]{:S(2)}, u32[]{:S(2)}) async-start(bf16[4,40,960]{2,1,0:T(8,128)(2,1)} %pad_maximum_fusion.9), calls=%async_computation | async-start | bytes 655360 | tf_op jit(solution)/shard_map/all_to_all | solution.py:117
  8.8 10.4 %copy-start = (bf16[2,512,1280]{2,1,0:T(8,128)(2,1)S(1)}, bf16[2,512,1280]{2,1,0:T(8,128)(2,1)}, u32[]{:S(2)}) copy-start(bf16[2,512,1280]{2,1,0:T(8,128)(2,1)} %param.11) | copy-start | bytes 7864324
  17.8 4.0 %copy-start.12 = (bf16[4,40,896]{2,1,0:T(8,128)(2,1)S(1)}, bf16[4,40,896]{2,1,0:T(8,128)(2,1)}, u32[]{:S(2)}) copy-start(bf16[4,40,896]{2,1,0:T(8,128)(2,1)} %concatenate.72) | copy-start | bytes 860164
  29.8 48.3 %all-to-all-start.1 = ((bf16[4,40,1792]{2,1,0:T(8,128)(2,1)}), bf16[4,40,1792]{2,1,0:T(8,128)(2,1)S(1)}, u32[]{:S(2)}, u32[]{:S(2)}) async-start(bf16[4,40,1792]{2,1,0:T(8,128)(2,1)} %pad_maximum_fusion.2), calls=%async_computation.1 | async-start | bytes 1146880 | tf_op jit(solution)/shard_map/all_to_all | solution.py:129
  33.3 33.1 %collective-permute-start = (bf16[160,960]{1,0:T(8,128)(2,1)S(1)}, bf16[160,960]{1,0:T(8,128)(2,1)S(1)}, u32[]{:S(2)}, u32[]{:S(2)}) collective-permute-start(bf16[160,960]{1,0:T(8,128)(2,1)S(1)} %bitcast.210), channel_id=1, source_target_pairs={{0,4},{4,0},{8,12},{12,8},{16,20},{20,16},{24,28},{28,24},{1,5},{5... | collective-permute-start | bytes 921608 | tf_op jit(solution)/shard_map/ppermute | solution.py:57
  34.5 8.6 %collective-permute-start.1 = (bf16[160,960]{1,0:T(8,128)(2,1)S(1)}, bf16[160,960]{1,0:T(8,128)(2,1)S(1)}, u32[]{:S(2)}, u32[]{:S(2)}) collective-permute-start(bf16[160,960]{1,0:T(8,128)(2,1)S(1)} %bitcast.211), channel_id=1, source_target_pairs={{0,8},{4,12},{8,16},{12,20},{16,24},{20,28},{24,0},{28,4},{1,9},{5... | collective-permute-start | bytes 921608 | tf_op jit(solution)/shard_map/ppermute | solution.py:56
  35.8 27.5 %collective-permute-start.3 = (bf16[160,960]{1,0:T(8,128)(2,1)S(1)}, bf16[160,960]{1,0:T(8,128)(2,1)S(1)}, u32[]{:S(2)}, u32[]{:S(2)}) collective-permute-start(bf16[160,960]{1,0:T(8,128)(2,1)S(1)} %bitcast.212), channel_id=1, source_target_pairs={{0,16},{4,20},{8,24},{12,28},{16,0},{20,4},{24,8},{28,12},{1,17},{... | collective-permute-start | bytes 921608 | tf_op jit(solution)/shard_map/ppermute | solution.py:56
  36.8 29.3 %collective-permute-start.5 = (bf16[160,960]{1,0:T(8,128)(2,1)S(1)}, bf16[160,960]{1,0:T(8,128)(2,1)S(1)}, u32[]{:S(2)}, u32[]{:S(2)}) collective-permute-start(bf16[160,960]{1,0:T(8,128)(2,1)S(1)} %bitcast.213), channel_id=1, source_target_pairs={{0,24},{4,28},{8,0},{12,4},{16,8},{20,12},{24,16},{28,20},{1,25},{... | collective-permute-start | bytes 921608 | tf_op jit(solution)/shard_map/ppermute | solution.py:56
  43.1 23.3 %collective-permute-start.2 = (bf16[160,960]{1,0:T(8,128)(2,1)S(1)}, bf16[160,960]{1,0:T(8,128)(2,1)S(1)}, u32[]{:S(2)}, u32[]{:S(2)}) collective-permute-start(bf16[160,960]{1,0:T(8,128)(2,1)S(1)} %collective-permute-done.1), channel_id=1, source_target_pairs={{0,4},{4,0},{8,12},{12,8},{16,20},{20,16},{24,28},{28,24},{1,5},{5... | collective-permute-start | bytes 921608 | tf_op jit(solution)/shard_map/ppermute | solution.py:57
  63.3 7.7 %collective-permute-start.4 = (bf16[160,960]{1,0:T(8,128)(2,1)S(1)}, bf16[160,960]{1,0:T(8,128)(2,1)S(1)}, u32[]{:S(2)}, u32[]{:S(2)}) collective-permute-start(bf16[160,960]{1,0:T(8,128)(2,1)S(1)} %collective-permute-done.3), channel_id=1, source_target_pairs={{0,4},{4,0},{8,12},{12,8},{16,20},{20,16},{24,28},{28,24},{1,5},{5... | collective-permute-start | bytes 921608 | tf_op jit(solution)/shard_map/ppermute | solution.py:57
  66.1 11.9 %collective-permute-start.6 = (bf16[160,960]{1,0:T(8,128)(2,1)S(1)}, bf16[160,960]{1,0:T(8,128)(2,1)S(1)}, u32[]{:S(2)}, u32[]{:S(2)}) collective-permute-start(bf16[160,960]{1,0:T(8,128)(2,1)S(1)} %collective-permute-done.5), channel_id=1, source_target_pairs={{0,4},{4,0},{8,12},{12,8},{16,20},{20,16},{24,28},{28,24},{1,5},{5... | collective-permute-start | bytes 921608 | tf_op jit(solution)/shard_map/ppermute | solution.py:57
  78.1 7.1 %copy-start.8 = (bf16[4,40,1792]{2,1,0:T(8,128)(2,1)}, bf16[4,40,1792]{2,1,0:T(8,128)(2,1)S(1)}, u32[]{:S(2)}) copy-start(bf16[4,40,1792]{2,1,0:T(8,128)(2,1)S(1)} %all-to-all-done.1) | copy-start | bytes 1720324
  78.1 49.3 %collective-permute-start.7 = (bf16[40,1280]{1,0:T(8,128)(2,1)}, bf16[40,1280]{1,0:T(8,128)(2,1)}, u32[]{:S(2)}, u32[]{:S(2)}) collective-permute-start(bf16[40,1280]{1,0:T(8,128)(2,1)} %convert_element_type.102), channel_id=1, source_target_pairs={{0,4},{4,0},{8,12},{12,8},{16,20},{20,16},{24,28},{28,24},{1,5},{5... | collective-permute-start | bytes 307208 | tf_op jit(solution)/shard_map/ppermute | solution.py:57
  78.4 49.0 %collective-permute-start.8 = (bf16[40,1280]{1,0:T(8,128)(2,1)}, bf16[40,1280]{1,0:T(8,128)(2,1)}, u32[]{:S(2)}, u32[]{:S(2)}) collective-permute-start(bf16[40,1280]{1,0:T(8,128)(2,1)} %convert_element_type.102), channel_id=1, source_target_pairs={{0,8},{4,12},{8,16},{12,20},{16,24},{20,28},{24,0},{28,4},{1,9},{5... | collective-permute-start | bytes 307208 | tf_op jit(solution)/shard_map/ppermute | solution.py:56
  78.4 51.2 %collective-permute-start.10 = (bf16[40,1280]{1,0:T(8,128)(2,1)}, bf16[40,1280]{1,0:T(8,128)(2,1)}, u32[]{:S(2)}, u32[]{:S(2)}) collective-permute-start(bf16[40,1280]{1,0:T(8,128)(2,1)} %convert_element_type.102), channel_id=1, source_target_pairs={{0,16},{4,20},{8,24},{12,28},{16,0},{20,4},{24,8},{28,12},{1,17},{... | collective-permute-start | bytes 307208 | tf_op jit(solution)/shard_map/ppermute | solution.py:56
  81.5 55.9 %collective-permute-start.12 = (bf16[40,1280]{1,0:T(8,128)(2,1)}, bf16[40,1280]{1,0:T(8,128)(2,1)S(1)}, u32[]{:S(2)}, u32[]{:S(2)}) collective-permute-start(bf16[40,1280]{1,0:T(8,128)(2,1)} %convert_element_type.102), channel_id=1, source_target_pairs={{0,24},{4,28},{8,0},{12,4},{16,8},{20,12},{24,16},{28,20},{1,25},{... | collective-permute-start | bytes 307208 | tf_op jit(solution)/shard_map/ppermute | solution.py:56
  85.1 3.9 %copy-start.1 = (bf16[2,512,1280]{2,1,0:T(8,128)(2,1)S(1)}, bf16[2,512,1280]{2,1,0:T(8,128)(2,1)}, u32[]{:S(2)}) copy-start(bf16[2,512,1280]{2,1,0:T(8,128)(2,1)} %param.11) | copy-start | bytes 7864324
  89.0 1.9 copy-start.14
  89.0 1.9 copy-start.23
  91.0 1.2 copy-start.15
  91.0 1.2 copy-start.16
  92.2 4.5 %copy-start.24 = (f32[1280]{0:T(1024)S(1)}, f32[1280]{0:T(1024)}, u32[]{:S(2)}) copy-start(f32[1280]{0:T(1024)} %param.13) | copy-start | bytes 15364
  96.6 2.4 copy-start.10
  96.6 2.4 copy-start.11
  99.0 2.2 copy-start.18
  99.0 2.2 copy-start.20
  116.5 9.6 %copy-start.13 = (bf16[112,1280]{1,0:T(8,128)(2,1)S(1)}, bf16[112,1280]{1,0:T(8,128)(2,1)}, u32[]{:S(2)}) copy-start(bf16[112,1280]{1,0:T(8,128)(2,1)} %convert_element_type.103) | copy-start | bytes 860164
  117.4 122.6 %all-to-all-start.2 = ((bf16[4,256,320]{1,2,0:T(8,128)(2,1)}), bf16[4,256,320]{1,2,0:T(8,128)(2,1)S(1)}, u32[]{:S(2)}, u32[]{:S(2)}) async-start(bf16[4,256,320]{1,2,0:T(8,128)(2,1)} %copy.75), calls=%async_computation.2 | async-start | bytes 1310720 | tf_op jit(solution)/shard_map/all_to_all | solution.py:197
  124.8 29.4 %collective-permute-start.25 = (bf16[112,1280]{1,0:T(8,128)(2,1)}, bf16[112,1280]{1,0:T(8,128)(2,1)S(1)}, u32[]{:S(2)}, u32[]{:S(2)}) collective-permute-start(bf16[112,1280]{1,0:T(8,128)(2,1)} %convert_element_type.103), channel_id=1, source_target_pairs={{0,4},{4,0},{8,12},{12,8},{16,20},{20,16},{24,28},{28,24},{1,5},{5... | collective-permute-start | bytes 860168 | tf_op jit(solution)/shard_map/ppermute | solution.py:57
  126.1 1.1 copy-start.9
  126.2 1.1 copy-start.19
  127.3 28.6 %collective-permute-start.26 = (bf16[112,1280]{1,0:T(8,128)(2,1)S(1)}, bf16[112,1280]{1,0:T(8,128)(2,1)S(1)}, u32[]{:S(2)}, u32[]{:S(2)}) collective-permute-start(bf16[112,1280]{1,0:T(8,128)(2,1)S(1)} %copy-done.13), channel_id=1, source_target_pairs={{0,8},{4,12},{8,16},{12,20},{16,24},{20,28},{24,0},{28,4},{1,9},{5... | collective-permute-start | bytes 860168 | tf_op jit(solution)/shard_map/ppermute | solution.py:56
  127.4 7.8 %collective-permute-start.9 = (bf16[40,1280]{1,0:T(8,128)(2,1)}, bf16[40,1280]{1,0:T(8,128)(2,1)S(1)}, u32[]{:S(2)}, u32[]{:S(2)}) collective-permute-start(bf16[40,1280]{1,0:T(8,128)(2,1)} %collective-permute-done.8), channel_id=1, source_target_pairs={{0,4},{4,0},{8,12},{12,8},{16,20},{20,16},{24,28},{28,24},{1,5},{5... | collective-permute-start | bytes 307208 | tf_op jit(solution)/shard_map/ppermute | solution.py:57
  129.6 26.7 %collective-permute-start.28 = (bf16[112,1280]{1,0:T(8,128)(2,1)S(1)}, bf16[112,1280]{1,0:T(8,128)(2,1)S(1)}, u32[]{:S(2)}, u32[]{:S(2)}) collective-permute-start(bf16[112,1280]{1,0:T(8,128)(2,1)S(1)} %copy-done.13), channel_id=1, source_target_pairs={{0,16},{4,20},{8,24},{12,28},{16,0},{20,4},{24,8},{28,12},{1,17},{... | collective-permute-start | bytes 860168 | tf_op jit(solution)/shard_map/ppermute | solution.py:56
  135.2 4.0 %collective-permute-start.11 = (bf16[40,1280]{1,0:T(8,128)(2,1)}, bf16[40,1280]{1,0:T(8,128)(2,1)S(1)}, u32[]{:S(2)}, u32[]{:S(2)}) collective-permute-start(bf16[40,1280]{1,0:T(8,128)(2,1)} %collective-permute-done.10), channel_id=1, source_target_pairs={{0,4},{4,0},{8,12},{12,8},{16,20},{20,16},{24,28},{28,24},{1,5},{5... | collective-permute-start | bytes 307208 | tf_op jit(solution)/shard_map/ppermute | solution.py:57
  137.4 75.1 %collective-permute-start.18 = (bf16[160,1792]{1,0:T(8,128)(2,1)S(1)}, bf16[160,1792]{1,0:T(8,128)(2,1)S(1)}, u32[]{:S(2)}, u32[]{:S(2)}) collective-permute-start(bf16[160,1792]{1,0:T(8,128)(2,1)S(1)} %bitcast.205), channel_id=1, source_target_pairs={{0,4},{4,0},{8,12},{12,8},{16,20},{20,16},{24,28},{28,24},{1,5},{5... | collective-permute-start | bytes 1720328 | tf_op jit(solution)/shard_map/ppermute | solution.py:57
  139.2 14.9 %collective-permute-start.13 = (bf16[40,1280]{1,0:T(8,128)(2,1)S(1)}, bf16[40,1280]{1,0:T(8,128)(2,1)S(1)}, u32[]{:S(2)}, u32[]{:S(2)}) collective-permute-start(bf16[40,1280]{1,0:T(8,128)(2,1)S(1)} %collective-permute-done.12), channel_id=1, source_target_pairs={{0,4},{4,0},{8,12},{12,8},{16,20},{20,16},{24,28},{28,24},{1,5},{5... | collective-permute-start | bytes 307208 | tf_op jit(solution)/shard_map/ppermute | solution.py:57
  154.1 58.7 %collective-permute-start.19 = (bf16[160,1792]{1,0:T(8,128)(2,1)S(1)}, bf16[160,1792]{1,0:T(8,128)(2,1)S(1)}, u32[]{:S(2)}, u32[]{:S(2)}) collective-permute-start(bf16[160,1792]{1,0:T(8,128)(2,1)S(1)} %bitcast.206), channel_id=1, source_target_pairs={{0,8},{4,12},{8,16},{12,20},{16,24},{20,28},{24,0},{28,4},{1,9},{5... | collective-permute-start | bytes 1720328 | tf_op jit(solution)/shard_map/ppermute | solution.py:56
  154.1 59.8 %collective-permute-start.21 = (bf16[160,1792]{1,0:T(8,128)(2,1)S(1)}, bf16[160,1792]{1,0:T(8,128)(2,1)}, u32[]{:S(2)}, u32[]{:S(2)}) collective-permute-start(bf16[160,1792]{1,0:T(8,128)(2,1)S(1)} %bitcast.207), channel_id=1, source_target_pairs={{0,16},{4,20},{8,24},{12,28},{16,0},{20,4},{24,8},{28,12},{1,17},{... | collective-permute-start | bytes 1720328 | tf_op jit(solution)/shard_map/ppermute | solution.py:56
  156.0 6.1 %collective-permute-start.27 = (bf16[112,1280]{1,0:T(8,128)(2,1)S(1)}, bf16[112,1280]{1,0:T(8,128)(2,1)S(1)}, u32[]{:S(2)}, u32[]{:S(2)}) collective-permute-start(bf16[112,1280]{1,0:T(8,128)(2,1)S(1)} %collective-permute-done.26), channel_id=1, source_target_pairs={{0,4},{4,0},{8,12},{12,8},{16,20},{20,16},{24,28},{28,24},{1,5},{5... | collective-permute-start | bytes 860168 | tf_op jit(solution)/shard_map/ppermute | solution.py:57
  156.3 58.0 %collective-permute-start.23 = (bf16[160,1792]{1,0:T(8,128)(2,1)S(1)}, bf16[160,1792]{1,0:T(8,128)(2,1)}, u32[]{:S(2)}, u32[]{:S(2)}) collective-permute-start(bf16[160,1792]{1,0:T(8,128)(2,1)S(1)} %bitcast.208), channel_id=1, source_target_pairs={{0,24},{4,28},{8,0},{12,4},{16,8},{20,12},{24,16},{28,20},{1,25},{... | collective-permute-start | bytes 1720328 | tf_op jit(solution)/shard_map/ppermute | solution.py:56
  162.1 5.8 %collective-permute-start.29 = (bf16[112,1280]{1,0:T(8,128)(2,1)S(1)}, bf16[112,1280]{1,0:T(8,128)(2,1)S(1)}, u32[]{:S(2)}, u32[]{:S(2)}) collective-permute-start(bf16[112,1280]{1,0:T(8,128)(2,1)S(1)} %collective-permute-done.28), channel_id=1, source_target_pairs={{0,4},{4,0},{8,12},{12,8},{16,20},{20,16},{24,28},{28,24},{1,5},{5... | collective-permute-start | bytes 860168 | tf_op jit(solution)/shard_map/ppermute | solution.py:57
  167.9 44.5 %collective-permute-start.30 = (bf16[112,1280]{1,0:T(8,128)(2,1)S(1)}, bf16[112,1280]{1,0:T(8,128)(2,1)S(1)}, u32[]{:S(2)}, u32[]{:S(2)}) collective-permute-start(bf16[112,1280]{1,0:T(8,128)(2,1)S(1)} %copy-done.13), channel_id=1, source_target_pairs={{0,24},{4,28},{8,0},{12,4},{16,8},{20,12},{24,16},{28,20},{1,25},{... | collective-permute-start | bytes 860168 | tf_op jit(solution)/shard_map/ppermute | solution.py:56
  212.4 19.3 %collective-permute-start.14 = (bf16[8,40,1280]{2,1,0:T(8,128)(2,1)S(1)}, bf16[8,40,1280]{2,1,0:T(8,128)(2,1)S(1)}, u32[]{:S(2)}, u32[]{:S(2)}) collective-permute-start(bf16[8,40,1280]{2,1,0:T(8,128)(2,1)S(1)} %bitcast.183), channel_id=1, source_target_pairs={{0,2},{1,3},{2,0},{3,1},{4,6},{5,7},{6,4},{7,5},{8,10},{9,11},{10,... | collective-permute-start | bytes 2457608 | tf_op jit(solution)/shard_map/ppermute | solution.py:41
  212.5 20.9 %collective-permute-start.31 = (bf16[112,1280]{1,0:T(8,128)(2,1)S(1)}, bf16[112,1280]{1,0:T(8,128)(2,1)S(1)}, u32[]{:S(2)}, u32[]{:S(2)}) collective-permute-start(bf16[112,1280]{1,0:T(8,128)(2,1)S(1)} %collective-permute-done.30), channel_id=1, source_target_pairs={{0,4},{4,0},{8,12},{12,8},{16,20},{20,16},{24,28},{28,24},{1,5},{5... | collective-permute-start | bytes 860168 | tf_op jit(solution)/shard_map/ppermute | solution.py:57
  212.8 20.9 %collective-permute-start.20 = (bf16[160,1792]{1,0:T(8,128)(2,1)S(1)}, bf16[160,1792]{1,0:T(8,128)(2,1)S(1)}, u32[]{:S(2)}, u32[]{:S(2)}) collective-permute-start(bf16[160,1792]{1,0:T(8,128)(2,1)S(1)} %collective-permute-done.19), channel_id=1, source_target_pairs={{0,4},{4,0},{8,12},{12,8},{16,20},{20,16},{24,28},{28,24},{1,5},{5... | collective-permute-start | bytes 1720328 | tf_op jit(solution)/shard_map/ppermute | solution.py:57
  214.0 30.8 %collective-permute-start.22 = (bf16[160,1792]{1,0:T(8,128)(2,1)}, bf16[160,1792]{1,0:T(8,128)(2,1)}, u32[]{:S(2)}, u32[]{:S(2)}) collective-permute-start(bf16[160,1792]{1,0:T(8,128)(2,1)} %collective-permute-done.21), channel_id=1, source_target_pairs={{0,4},{4,0},{8,12},{12,8},{16,20},{20,16},{24,28},{28,24},{1,5},{5... | collective-permute-start | bytes 1720328 | tf_op jit(solution)/shard_map/ppermute | solution.py:57
  214.3 48.8 %collective-permute-start.24 = (bf16[160,1792]{1,0:T(8,128)(2,1)}, bf16[160,1792]{1,0:T(8,128)(2,1)}, u32[]{:S(2)}, u32[]{:S(2)}) collective-permute-start(bf16[160,1792]{1,0:T(8,128)(2,1)} %collective-permute-done.23), channel_id=1, source_target_pairs={{0,4},{4,0},{8,12},{12,8},{16,20},{20,16},{24,28},{28,24},{1,5},{5... | collective-permute-start | bytes 1720328 | tf_op jit(solution)/shard_map/ppermute | solution.py:57
  232.0 4.5 %collective-permute-start.15 = (bf16[2,8,40,1280]{3,2,1,0:T(8,128)(2,1)S(1)}, bf16[2,8,40,1280]{3,2,1,0:T(8,128)(2,1)S(1)}, u32[]{:S(2)}, u32[]{:S(2)}) collective-permute-start(bf16[2,8,40,1280]{3,2,1,0:T(8,128)(2,1)S(1)} %maximum_select_fusion.4), channel_id=1, source_target_pairs={{0,1},{1,0},{2,3},{3,2},{4,5},{5,4},{6,7},{7,6},{8,9},{9,8},{10,11... | collective-permute-start | bytes 4915208 | tf_op jit(solution)/shard_map/ppermute | solution.py:41
  233.4 1.9 copy-start.7
  235.4 2.2 copy-start.3
  240.0 3.5 %copy-start.21 = (f32[1280]{0:T(1024)S(1)}, f32[1280]{0:T(1024)}, u32[]{:S(2)}) copy-start(f32[1280]{0:T(1024)} %param.14) | copy-start | bytes 15364
  243.7 15.2 %collective-permute-start.16 = (bf16[256,1280]{1,0:T(8,128)(2,1)S(1)}, bf16[256,1280]{1,0:T(8,128)(2,1)S(1)}, u32[]{:S(2)}, u32[]{:S(2)}) collective-permute-start(bf16[256,1280]{1,0:T(8,128)(2,1)S(1)} %multiply_convert_fusion.3), channel_id=1, source_target_pairs={{0,2},{1,3},{2,0},{3,1},{4,6},{5,7},{6,4},{7,5},{8,10},{9,11},{10,... | collective-permute-start | bytes 1966088 | tf_op jit(solution)/shard_map/ppermute | solution.py:41
  259.1 6.4 %collective-permute-start.17 = (bf16[2,256,1280]{2,1,0:T(8,128)(2,1)S(1)}, bf16[2,256,1280]{2,1,0:T(8,128)(2,1)S(1)}, u32[]{:S(2)}, u32[]{:S(2)}) collective-permute-start(bf16[2,256,1280]{2,1,0:T(8,128)(2,1)S(1)} %maximum_select_fusion.5), channel_id=1, source_target_pairs={{0,1},{1,0},{2,3},{3,2},{4,5},{5,4},{6,7},{7,6},{8,9},{9,8},{10,11... | collective-permute-start | bytes 3932168 | tf_op jit(solution)/shard_map/ppermute | solution.py:41
  266.1 7.3 %copy-start.4 = (bf16[2,2,256,1280]{3,2,1,0:T(8,128)(2,1)}, bf16[2,2,256,1280]{3,2,1,0:T(8,128)(2,1)S(1)}, u32[]{:S(2)}) copy-start(bf16[2,2,256,1280]{3,2,1,0:T(8,128)(2,1)S(1)} %copy.79) | copy-start | bytes 7864324
  287.2 3.4 %collective-permute-start.32 = (bf16[2,256,1280]{2,1,0:T(8,128)(2,1)}, bf16[2,256,1280]{2,1,0:T(8,128)(2,1)}, u32[]{:S(2)}, u32[]{:S(2)}) collective-permute-start(bf16[2,256,1280]{2,1,0:T(8,128)(2,1)} %dynamic-slice_bitcast_fusion), channel_id=1, source_target_pairs={{0,1},{1,0},{2,3},{3,2},{4,5},{5,4},{6,7},{7,6},{8,9},{9,8},{10,11... | collective-permute-start | bytes 3932168 | tf_op jit(solution)/shard_map/ppermute | solution.py:41
  292.6 1.5 copy-start.2
  294.1 16.4 %collective-permute-start.33 = (bf16[256,1280]{1,0:T(8,128)(2,1)S(1)}, bf16[256,1280]{1,0:T(8,128)(2,1)}, u32[]{:S(2)}, u32[]{:S(2)}) collective-permute-start(bf16[256,1280]{1,0:T(8,128)(2,1)S(1)} %fusion.27), channel_id=1, source_target_pairs={{0,2},{1,3},{2,0},{3,1},{4,6},{5,7},{6,4},{7,5},{8,10},{9,11},{10,... | collective-permute-start | bytes 1966088 | tf_op jit(solution)/shard_map/ppermute | solution.py:41
  312.2 15.3 %collective-permute-start.34 = (bf16[256,1280]{1,0:T(8,128)(2,1)S(1)}, bf16[256,1280]{1,0:T(8,128)(2,1)S(1)}, u32[]{:S(2)}, u32[]{:S(2)}) collective-permute-start(bf16[256,1280]{1,0:T(8,128)(2,1)S(1)} %fusion.21), channel_id=1, source_target_pairs={{0,2},{1,3},{2,0},{3,1},{4,6},{5,7},{6,4},{7,5},{8,10},{9,11},{10,... | collective-permute-start | bytes 1966088 | tf_op jit(solution)/shard_map/ppermute | solution.py:41
  327.6 3.1 copy-start.5
  328.8 4.9 %collective-permute-start.35 = (bf16[2,256,1280]{2,1,0:T(8,128)(2,1)}, bf16[2,256,1280]{2,1,0:T(8,128)(2,1)}, u32[]{:S(2)}, u32[]{:S(2)}) collective-permute-start(bf16[2,256,1280]{2,1,0:T(8,128)(2,1)} %maximum_select_fusion.7), channel_id=1, source_target_pairs={{0,1},{1,0},{2,3},{3,2},{4,5},{5,4},{6,7},{7,6},{8,9},{9,8},{10,11... | collective-permute-start | bytes 3932168 | tf_op jit(solution)/shard_map/ppermute | solution.py:41
  331.4 1.5 copy-start.6

commit v3 on v2

--- a/solution.py
+++ b/solution.py
@@ -41,24 +41,33 @@
     return lax.ppermute(field, "tp", [(s, s ^ flip) for s in range(lax.axis_size("tp"))])
 
 
-def gather_req(shard):
+def gather_far(shard):
     count = lax.axis_size("req")
-    inner = 2
-    outer = count // inner
+    held = [shard]
+    for step in range(2, count, 2):
+        pairs = [(r, (r + step) % count) for r in range(count)]
+        held.append(lax.ppermute(shard, "req", pairs))
+    return held
+
+
+def gather_near(held):
+    count = lax.axis_size("req")
+    outer = len(held)
+    shape = held[0].shape
     me = lax.axis_index("req")
-    far, near = me // inner, me % inner
-    out = jnp.zeros((outer, inner) + shard.shape, shard.dtype)
-    zeros = (0,) * shard.ndim
-    for step in range(outer):
-        held = shard
-        if step:
-            pairs = [(r, (r + step * inner) % count) for r in range(count)]
-            held = lax.ppermute(shard, "req", pairs)
-        other = lax.ppermute(held, "req", [(r, r ^ 1) for r in range(count)])
+    far, near = me // 2, me % 2
+    out = jnp.zeros((outer, 2) + shape, held[0].dtype)
+    zeros = (0,) * len(shape)
+    swapped = [lax.ppermute(mine, "req", [(r, r ^ 1) for r in range(count)]) for mine in held]
+    for step, (mine, other) in enumerate(zip(held, swapped)):
         place = (far + outer - step) % outer
-        out = lax.dynamic_update_slice(out, held[None, None], (place, near) + zeros)
+        out = lax.dynamic_update_slice(out, mine[None, None], (place, near) + zeros)
         out = lax.dynamic_update_slice(out, other[None, None], (place, 1 - near) + zeros)
-    return out.reshape((count,) + shard.shape)
+    return out.reshape((count,) + shape)
+
+
+def tie(*fields):
+    return lax.optimization_barrier(fields)
 
 
 def gather_tp(rows):
@@ -115,7 +124,14 @@
     first_pack = jnp.concatenate([q_parts, kv_parts], axis=2).astype(half)
     first_pack = first_pack.reshape(tp_count * shard_rows, q_cols + 2 * kv_cols)
     first_pack = lax.all_to_all(first_pack, "tp", 0, 0, tiled=True)
-    first_full = gather_req(first_pack).reshape(-1, q_cols + 2 * kv_cols)
+    first_pack, gate_master, up_master, o_master, down_master = tie(
+        first_pack, gate_master, up_master, o_master, down_master
+    )
+    first_far = gather_far(first_pack)
+    third_pack = jnp.concatenate([o_master, down_master]).astype(half)
+    first_far, third_pack = tie(first_far, third_pack)
+    third_far = gather_far(third_pack)
+    first_full = gather_near(first_far).reshape(-1, q_cols + 2 * kv_cols)
 
     def ff_parts(master):
         return (
@@ -127,18 +143,9 @@
 
     second_pack = jnp.concatenate([ff_parts(gate_master), ff_parts(up_master)], axis=1)
     second_pack = lax.all_to_all(second_pack, "tp", 0, 0, tiled=True)
-    first_full, second_pack, o_own, down_own = lax.optimization_barrier(
-        (first_full, second_pack, o_master.astype(half), down_master.astype(half))
-    )
-    o_full = gather_tp(gather_req(o_own)).transpose(1, 0, 2, 3).reshape(-1, o_own.shape[1])
-    second_full = gather_req(second_pack).reshape(-1, 2 * ff_cols)
-    down_weight = gather_req(down_own).reshape(ff_cols, down_own.shape[1])
-
     query_weight = first_full[:, :q_cols]
     key_weight = first_full[:, q_cols : q_cols + kv_cols]
     value_weight = first_full[:, q_cols + kv_cols :]
-    gate_weight = second_full[:, :ff_cols]
-    up_weight = second_full[:, ff_cols:]
     prompt_batch, sequence_length, model_width = hidden_in.shape
     tok_rows = prompt_batch * sequence_length
     flat_rows = hidden_in.reshape(tok_rows, model_width).astype(jnp.float32)
@@ -153,6 +160,11 @@
     value_rows = jnp.dot(
         normalized_input, value_weight, preferred_element_type=jnp.float32
     ).reshape(prompt_batch, sequence_length, KEY_VALUE_HEADS, HEAD_DIM)
+    queries, key_rows, value_rows, third_far, second_pack = tie(
+        queries, key_rows, value_rows, third_far, second_pack
+    )
+    second_far = gather_far(second_pack)
+    third_full = gather_near(third_far)
     cosine_table, sine_table = rope_tables(sequence_length, HEAD_DIM)
     q_rot = rotate(queries, cosine_table, sine_table).astype(jnp.bfloat16)
     rotated_keys = rotate(key_rows, cosine_table, sine_table).astype(jnp.bfloat16)
@@ -193,18 +205,32 @@
         .astype(jnp.bfloat16)
         .reshape(tok_rows, local_heads * HEAD_DIM)
     )
+    attended, second_far, third_full = tie(attended, second_far, third_full)
+    second_full = gather_near(second_far).reshape(-1, 2 * ff_cols)
+    o_own, down_weight = third_full[:, :shard_rows], third_full[:, shard_rows:]
+    down_weight = down_weight.reshape(ff_cols, model_width)
+    o_full = gather_tp(o_own).transpose(1, 0, 2, 3).reshape(-1, model_width)
+    gate_weight = second_full[:, :ff_cols]
+    up_weight = second_full[:, ff_cols:]
     own_rows = tok_rows // tp_count
     attended_rows = lax.all_to_all(attended, "tp", 0, 1, tiled=True)
     own_hidden = lax.dynamic_slice_in_dim(flat_rows, tensor_shard_index * own_rows, own_rows, 0)
     middle = own_hidden + jnp.dot(attended_rows, o_full, preferred_element_type=jnp.float32)
-    normed_rows = gather_tp(rms_norm(middle, mlp_gain)).reshape(tok_rows, model_width)
-    gate_val = jnp.dot(normed_rows, gate_weight, preferred_element_type=jnp.float32)
-    up_val = jnp.dot(normed_rows, up_weight, preferred_element_type=jnp.float32)
-    hidden_ff = (jax.nn.silu(gate_val) * up_val).astype(jnp.bfloat16)
-    ffn_rows = scatter_tp(
-        jnp.dot(hidden_ff, down_weight, preferred_element_type=jnp.float32).astype(jnp.bfloat16)
-    )
-    result = gather_tp((middle + ffn_rows).astype(jnp.bfloat16))
+    normed_rows = gather_tp(rms_norm(middle, mlp_gain))
+    results = []
+    for chunk in range(2):
+        part = slice(chunk * own_rows // 2, (chunk + 1) * own_rows // 2)
+        rows = normed_rows[:, part].reshape(tok_rows // 2, model_width)
+        gate_val = jnp.dot(rows, gate_weight, preferred_element_type=jnp.float32)
+        up_val = jnp.dot(rows, up_weight, preferred_element_type=jnp.float32)
+        hidden_ff = (jax.nn.silu(gate_val) * up_val).astype(jnp.bfloat16)
+        sums = scatter_tp(
+            jnp.dot(hidden_ff, down_weight, preferred_element_type=jnp.float32).astype(
+                jnp.bfloat16
+            )
+        )
+        results.append(gather_tp((middle[part] + sums).astype(jnp.bfloat16)))
+    result = jnp.concatenate(results, axis=1)
     return (result.reshape(prompt_batch, sequence_length, model_width), kv_cache)
 
 

time: 339 us -> 294 us (0.87)
  waiting for transfers between devices: 179 us -> 109 us
  local copies, waits for them, and re-layouts: 39.9 us -> 48.4 us
  matrix products: 43.9 us -> 50.7 us
  starting transfers between devices: 42.9 us -> 49.2 us
    ppermute x28 -> x21, waiting for transfers between devices: 114 us -> 56.3 us  [the longest x12 43.1 us: gather_near(): lax.ppermute(mine, 'req', [(r, r ^ 1) for r in range(count)])]
    ppermute x8 -> x12, waiting for transfers between devices: 64.6 us -> 52.5 us  [tp_permute(): lax.ppermute(field, 'tp', [(s, s ^ flip) for s in range(lax.axis_size('tp...]
    ppermute x8 -> x12, starting transfers between devices: 5.89 us -> 13.5 us  [tp_permute(): lax.ppermute(field, 'tp', [(s, s ^ flip) for s in range(lax.axis_size('tp...]
    dynamic_update_slice x32 -> x24, local copies, waits for them, and re-layouts: 10.8 us -> 16.1 us  [the longest x12 11.6 us: gather_near(): out = lax.dynamic_update_slice(out, mine[None, None], (place, near) + zeros)]
    ppermute x28 -> x21, starting transfers between devices: 21.9 us -> 17.9 us  [the longest x9 9.93 us: gather_far(): held.append(lax.ppermute(shard, 'req', pairs))]
    dot_general x1 -> x2, matrix products: 11.4 us -> 14.8 us  [local(): jnp.dot(hidden_ff, down_weight, preferred_element_type=jnp.float32)]
    convert_element_type x3 -> x1, other arithmetic: 5.09 us -> 1.67 us  [local(): results.append(gather_tp((middle[part] + sums).astype(jnp.bfloat16)))]
    concatenate x0 -> x2, other arithmetic: none -> 3.41 us  [the longest x1 1.75 us: local(): third_pack = jnp.concatenate([o_master, down_master]).astype(half)]
  transfers between devices with their start and end apart: 39 -> 36, of which waited for: 19 -> 17; matrix products, arithmetic and copies ran while one was open for 23% -> 37% of each run, Pallas kernels for 0% -> 0%
where the time goes in v3:
time: 294 us; the launch traced here: 289 us
  waiting for transfers between devices  109 us (37%)
  matrix products  50.7 us (17%)
  starting transfers between devices  49.2 us (17%)
  local copies, waits for them, and re-layouts  48.4 us (16%)
  other arithmetic  31.1 us (11%)
    ppermute x12, waiting for transfers between devices, tp_permute(): lax.ppermute(field, 'tp', [(s, s ^ flip) for s in range(lax.axis_size('tp...  52.5 us
    ppermute x12, waiting for transfers between devices, gather_near(): lax.ppermute(mine, 'req', [(r, r ^ 1) for r in range(count)])  43.1 us
    dot_general x2, matrix products, local(): jnp.dot(hidden_ff, down_weight, preferred_element_type=jnp.float32)  14.8 us
    ppermute x12, starting transfers between devices, tp_permute(): lax.ppermute(field, 'tp', [(s, s ^ flip) for s in range(lax.axis_size('tp...  13.5 us
    ppermute x9, waiting for transfers between devices, gather_far(): held.append(lax.ppermute(shard, 'req', pairs))  13.2 us
    dynamic_update_slice x12, local copies, waits for them, and re-layouts, gather_near(): out = lax.dynamic_update_slice(out, mine[None, None], (place, near) + zeros)  11.6 us
    ppermute x9, starting transfers between devices, gather_far(): held.append(lax.ppermute(shard, 'req', pairs))  9.93 us
    sub x1, matrix products, local(): expo = jnp.exp(scores - highest)  9.42 us
  transfers between devices with their start and end apart: 36, of which 17 were waited for; matrix products, arithmetic and copies ran while one was open for 37% of the time, Pallas kernels for 0%

profile of v3, /device:TPU:13, one launch (start us, length us, event | category | flops | bytes accessed | tf_op | source)
XLA Modules:
  0.0 289.4 jit_solution(16545942772802449124)
XLA Ops:
  3.8 4.2 %all-to-all-start = ((bf16[4,40,960]{2,1,0:T(8,128)(2,1)}), bf16[4,40,960]{2,1,0:T(8,128)(2,1)S(1)}, u32[]{:S(2)}, u32[]{:S(2)}) async-start(bf16[4,40,960]{2,1,0:T(8,128)(2,1)} %pad_maximum_fusion.11), calls=%async_computation | async-start | bytes 655360 | tf_op jit(solution)/shard_map/all_to_all | solution.py:126
  10.0 2.7 convert.37
  13.0 1.3 collective-permute-start
  15.4 1.4 collective-permute-start.2
  16.8 1.8 convert.27
  18.7 1.8 convert_element_type.123
  20.5 1.4 reshape.498
  22.6 2.0 concatenate.94
  24.6 1.8 convert_element_type.122
  26.4 1.4 reshape.497
  28.6 1.3 concatenate.93
  29.8 1.7 pad_maximum_fusion.10
  31.6 10.5 %collective-permute-done.1 = bf16[160,960]{1,0:T(8,128)(2,1)} collective-permute-done((bf16[160,960]{1,0:T(8,128)(2,1)S(1)}, bf16[160,960]{1,0:T(8,128)(2,1)}, u32[]{:S(2)}, u32[]{:S(2)}) %collective-permute-start.1) | collective-permute-done | bytes 307232 | tf_op jit(solution)/shard_map/ppermute | solution.py:49
  42.1 2.7 collective-permute-done.2
  46.0 1.8 pad_maximum_fusion.3
  47.8 5.7 %all-to-all-start.1 = ((bf16[4,40,1792]{2,1,0:T(8,128)(2,1)}), bf16[4,40,1792]{2,1,0:T(8,128)(2,1)}, u32[]{:S(2)}, u32[]{:S(2)}) async-start(bf16[4,40,1792]{2,1,0:T(8,128)(2,1)} %pad_maximum_fusion.3), calls=%async_computation.1 | async-start | bytes 1146880 | tf_op jit(solution)/shard_map/all_to_all | solution.py:145
  53.5 1.3 collective-permute-start.8
  54.8 1.5 collective-permute-start.9
  56.9 1.3 collective-permute-start.5
  60.2 4.4 %collective-permute-done.4 = bf16[160,960]{1,0:T(8,128)(2,1)S(1)} collective-permute-done((bf16[160,960]{1,0:T(8,128)(2,1)}, bf16[160,960]{1,0:T(8,128)(2,1)S(1)}, u32[]{:S(2)}, u32[]{:S(2)}) %collective-permute-start.4) | collective-permute-done | bytes 307232 | tf_op jit(solution)/shard_map/ppermute | solution.py:61
  65.9 5.7 %collective-permute-done.5 = bf16[160,960]{1,0:T(8,128)(2,1)S(1)} collective-permute-done((bf16[160,960]{1,0:T(8,128)(2,1)}, bf16[160,960]{1,0:T(8,128)(2,1)S(1)}, u32[]{:S(2)}, u32[]{:S(2)}) %collective-permute-start.5) | collective-permute-done | bytes 307232 | tf_op jit(solution)/shard_map/ppermute | solution.py:61
  72.7 5.9 %collective-permute-done.6 = bf16[160,960]{1,0:T(8,128)(2,1)S(1)} collective-permute-done((bf16[160,960]{1,0:T(8,128)(2,1)}, bf16[160,960]{1,0:T(8,128)(2,1)S(1)}, u32[]{:S(2)}, u32[]{:S(2)}) %collective-permute-start.6) | collective-permute-done | bytes 307232 | tf_op jit(solution)/shard_map/ppermute | solution.py:61
  78.6 2.2 slice_bitcast_fusion
  80.7 2.2 copy.46
  82.9 2.2 copy.48
  85.2 2.3 fusion.44
  87.5 2.2 fusion.48
  89.7 2.2 copy.47
  91.9 3.3 %fusion.46 = f32[2,512,5,64]{1,3,2,0:T(8,128)} fusion(bf16[5,64,1280,1]{2,1,0,3:T(8,128)(2,1)} %bitcast.247, bf16[2,512,1280]{2,1,0:T(8,128)(2,1)S(1)} %copy-done, f32[1280]{0:T(1024)S(1)} %copy-done.16, f32[2,512]{1,0:T(2,128)S(1)} %add_rsqrt_fusion), kind=kOutput, calls=%fused_computation.114 | convolution fusion | flops 844103680 | bytes 4760576 | tf_op jit(solution)/shard_map/dot_general | solution.py:157
  95.8 2.9 collective-permute-start.11
  98.6 2.2 subtract_convert_fusion
  101.1 1.5 fusion.20
  103.2 9.4 %fusion.66 = (f32[2,5,512]{2,1,0:T(8,128)S(1)}, f32[2,5,512,512]{2,3,1,0:T(8,128)}) fusion(pred[2,512,512]{1,2,0:T(8,128)(4,1)S(1)} %copy-done.11, bf16[2,512,5,32]{1,3,2,0:T(8,128)(2,1)} %get-tuple-element.61, bf16[2,512,5,32]{1,3,2,0:T(8,128)(2,1)S(1)} %get-tuple-element.60, bf16[2,512,5,64]{1,2,3,0:T(8,128)(2,1)} %fusion.20), kind=kOutput, calls=%fused_computation.141 | convolution fusion | flops 347341312 | bytes 12341248 | tf_op jit(solution)/shard_map/sub | solution.py:201
  112.7 5.0 %fusion.22 = bf16[2,512,5,64]{1,3,2,0:T(8,128)(2,1)S(1)} fusion(f32[2,5,512,512]{2,3,1,0:T(8,128)} %get-tuple-element.67, f32[2,5,512]{2,1,0:T(8,128)S(1)} %get-tuple-element.66, bf16[2,512,5,64]{1,2,3,0:T(8,128)(2,1)S(1)} %fusion.19), kind=kOutput, calls=%fused_computation.45 | convolution fusion | flops 341114880 | bytes 11816960 | tf_op jit(solution)/shard_map/phqk,pkhd->pqhd/dot_general | solution.py:204
  118.7 1.2 collective-permute-start.14
  121.2 5.8 %collective-permute-done.13 = bf16[152,1280]{1,0:T(8,128)(2,1)S(1)} collective-permute-done((bf16[152,1280]{1,0:T(8,128)(2,1)}, bf16[152,1280]{1,0:T(8,128)(2,1)S(1)}, u32[]{:S(2)}, u32[]{:S(2)}) %collective-permute-start.13) | collective-permute-done | bytes 389152 | tf_op jit(solution)/shard_map/ppermute | solution.py:61
  128.4 7.0 %collective-permute-done.14 = bf16[152,1280]{1,0:T(8,128)(2,1)S(1)} collective-permute-done((bf16[152,1280]{1,0:T(8,128)(2,1)}, bf16[152,1280]{1,0:T(8,128)(2,1)S(1)}, u32[]{:S(2)}, u32[]{:S(2)}) %collective-permute-start.14) | collective-permute-done | bytes 389152 | tf_op jit(solution)/shard_map/ppermute | solution.py:61
  136.6 7.2 %collective-permute-done.15 = bf16[152,1280]{1,0:T(8,128)(2,1)S(1)} collective-permute-done((bf16[152,1280]{1,0:T(8,128)(2,1)}, bf16[152,1280]{1,0:T(8,128)(2,1)S(1)}, u32[]{:S(2)}, u32[]{:S(2)}) %collective-permute-start.15) | collective-permute-done | bytes 389152 | tf_op jit(solution)/shard_map/ppermute | solution.py:61
  144.8 7.2 %collective-permute-done.16 = bf16[152,1280]{1,0:T(8,128)(2,1)S(1)} collective-permute-done((bf16[152,1280]{1,0:T(8,128)(2,1)}, bf16[152,1280]{1,0:T(8,128)(2,1)S(1)}, u32[]{:S(2)}, u32[]{:S(2)}) %collective-permute-start.16) | collective-permute-done | bytes 389152 | tf_op jit(solution)/shard_map/ppermute | solution.py:61
  153.4 1.5 slice.57
  155.8 7.8 %all-to-all-start.2 = ((bf16[4,256,320]{1,2,0:T(8,128)(2,1)}), bf16[4,256,320]{1,2,0:T(8,128)(2,1)}, u32[]{:S(2)}, u32[]{:S(2)}) async-start(bf16[4,256,320]{1,2,0:T(8,128)(2,1)} %bitcast.221), calls=%async_computation.2 | async-start | bytes 1310720 | tf_op jit(solution)/shard_map/all_to_all | solution.py:216
  168.9 20.7 %collective-permute-done.17 = bf16[8,40,1280]{2,1,0:T(8,128)(2,1)S(1)} collective-permute-done((bf16[8,40,1280]{2,1,0:T(8,128)(2,1)}, bf16[8,40,1280]{2,1,0:T(8,128)(2,1)S(1)}, u32[]{:S(2)}, u32[]{:S(2)}) %collective-permute-start.17) | collective-permute-done | bytes 819232 | tf_op jit(solution)/shard_map/ppermute | solution.py:41
  193.6 1.2 copy-done.1
  195.4 2.0 copy.58
  197.4 3.8 %multiply_reduce_fusion.1 = (f32[256]{0:T(256)S(1)}, f32[256,1280]{1,0:T(8,128)S(1)}) fusion(bf16[256,1280]{0,1:T(8,128)(2,1)} %bitcast.43, bf16[1280,1280]{1,0:T(8,128)(2,1)} %bitcast.196, f32[1024,1280]{1,0:T(8,128)} %convert.37, s32[]{:T(128)S(6)} %select_n.283), kind=kOutput, calls=%fused_computation.44 | convolution fusion | flops 839843584 | bytes 6554628 | tf_op jit(solution)/shard_map/dot_general | solution.py:218
  201.4 1.5 collective-permute-start.19
  204.1 13.6 %collective-permute-done.19 = bf16[256,1280]{1,0:T(8,128)(2,1)S(1)} collective-permute-done((bf16[256,1280]{1,0:T(8,128)(2,1)S(1)}, bf16[256,1280]{1,0:T(8,128)(2,1)S(1)}, u32[]{:S(2)}, u32[]{:S(2)}) %collective-permute-start.19) | collective-permute-done | bytes 655392 | tf_op jit(solution)/shard_map/ppermute | solution.py:41
  222.4 1.3 fusion.65
  223.7 2.8 fusion.13
  226.5 7.4 %convolution_convert_fusion.1 = bf16[512,1280]{1,0:T(8,128)(2,1)} fusion(bf16[896,1280]{1,0:T(8,128)(2,1)} %bitcast.225, f32[512,896]{1,0:T(8,128)} %fusion.13, bf16[512,1280]{1,0:T(8,128)(2,1)} %bitcast.231, bf16[1280,1792]{1,0:T(8,128)(2,1)} %bitcast.209), kind=kOutput, calls=%fused_computation.13 | convolution fusion | flops 2352218112 | bytes 9043968 | tf_op jit(solution)/shard_map/dot_general | solution.py:228
  235.4 4.8 %fusion.11 = f32[512,896]{1,0:T(8,128)} fusion(bf16[512,1280]{1,0:T(8,128)(2,1)} %bitcast.228, bf16[1280,1792]{1,0:T(8,128)(2,1)} %bitcast.210), kind=kOutput, calls=%fused_computation.22 | convolution fusion | flops 1174405120 | bytes 5439488 | tf_op jit(solution)/shard_map/dot_general | solution.py:224
  240.2 7.4 %convolution_convert_fusion = bf16[512,1280]{1,0:T(8,128)(2,1)} fusion(bf16[896,1280]{1,0:T(8,128)(2,1)} %bitcast.226, f32[512,896]{1,0:T(8,128)} %fusion.11, bf16[512,1280]{1,0:T(8,128)(2,1)} %bitcast.229, bf16[1280,1792]{1,0:T(8,128)(2,1)} %bitcast.211), kind=kOutput, calls=%fused_computation.12 | convolution fusion | flops 2352218112 | bytes 9043968 | tf_op jit(solution)/shard_map/dot_general | solution.py:228
  247.7 1.2 dynamic-slice_bitcast_fusion
  250.5 1.5 collective-permute-start.26
  254.8 4.7 %collective-permute-done.26 = bf16[128,1280]{1,0:T(8,128)(2,1)S(1)} collective-permute-done((bf16[128,1280]{1,0:T(8,128)(2,1)S(1)}, bf16[128,1280]{1,0:T(8,128)(2,1)S(1)}, u32[]{:S(2)}, u32[]{:S(2)}) %collective-permute-start.26) | collective-permute-done | bytes 327712 | tf_op jit(solution)/shard_map/ppermute | solution.py:41
  260.2 6.4 %collective-permute-done.30 = bf16[128,1280]{1,0:T(8,128)(2,1)} collective-permute-done((bf16[128,1280]{1,0:T(8,128)(2,1)}, bf16[128,1280]{1,0:T(8,128)(2,1)}, u32[]{:S(2)}, u32[]{:S(2)}) %collective-permute-start.30) | collective-permute-done | bytes 327712 | tf_op jit(solution)/shard_map/ppermute | solution.py:41
  266.6 1.7 fusion.34
  268.3 1.5 collective-permute-start.31
  270.6 1.5 pad_maximum_fusion.1
  272.1 4.4 %collective-permute-done.31 = bf16[128,1280]{1,0:T(8,128)(2,1)} collective-permute-done((bf16[128,1280]{1,0:T(8,128)(2,1)S(1)}, bf16[128,1280]{1,0:T(8,128)(2,1)}, u32[]{:S(2)}, u32[]{:S(2)}) %collective-permute-start.31) | collective-permute-done | bytes 327712 | tf_op jit(solution)/shard_map/ppermute | solution.py:41
  277.7 3.8 %collective-permute-start.32 = (bf16[2,128,1280]{2,1,0:T(8,128)(2,1)S(1)}, bf16[2,128,1280]{2,1,0:T(8,128)(2,1)S(1)}, u32[]{:S(2)}, u32[]{:S(2)}) collective-permute-start(bf16[2,128,1280]{2,1,0:T(8,128)(2,1)S(1)} %maximum_select_fusion.10), channel_id=1, source_target_pairs={{0,1},{1,0},{2,3},{3,2},{4,5},{5,4},{6,7},{7,6},{8,9},{9,8},{10,11... | collective-permute-start | bytes 1966088 | tf_op jit(solution)/shard_map/ppermute | solution.py:41
  281.5 1.9 collective-permute-done.27
  283.6 2.1 collective-permute-start.28
  287.7 1.7 pad_maximum_fusion
  (157 shorter events, 50.2 us)
Async XLA Ops:
  0.6 7.6 %copy-start.15 = (s32[2]{0:T(128)S(1)}, s32[2]{0:T(128)}, u32[]{:S(2)}) copy-start(s32[2]{0:T(128)} %param.12) | copy-start | bytes 28
  0.6 7.6 %copy-start = (bf16[2,512,1280]{2,1,0:T(8,128)(2,1)S(1)}, bf16[2,512,1280]{2,1,0:T(8,128)(2,1)}, u32[]{:S(2)}) copy-start(bf16[2,512,1280]{2,1,0:T(8,128)(2,1)} %param.11) | copy-start | bytes 7864324
  3.8 9.2 %all-to-all-start = ((bf16[4,40,960]{2,1,0:T(8,128)(2,1)}), bf16[4,40,960]{2,1,0:T(8,128)(2,1)S(1)}, u32[]{:S(2)}, u32[]{:S(2)}) async-start(bf16[4,40,960]{2,1,0:T(8,128)(2,1)} %pad_maximum_fusion.11), calls=%async_computation | async-start | bytes 655360 | tf_op jit(solution)/shard_map/all_to_all | solution.py:126
  10.0 8.6 %copy-start.13 = (f32[40,1280]{1,0:T(8,128)S(1)}, f32[40,1280]{1,0:T(8,128)}, u32[]{:S(2)}) copy-start(f32[40,1280]{1,0:T(8,128)} %param.18) | copy-start | bytes 614404
  13.0 18.6 %collective-permute-start = (bf16[160,960]{1,0:T(8,128)(2,1)S(1)}, bf16[160,960]{1,0:T(8,128)(2,1)}, u32[]{:S(2)}, u32[]{:S(2)}) collective-permute-start(bf16[160,960]{1,0:T(8,128)(2,1)S(1)} %bitcast.232), channel_id=1, source_target_pairs={{0,8},{4,12},{8,16},{12,20},{16,24},{20,28},{24,0},{28,4},{1,9},{5... | collective-permute-start | bytes 921608 | tf_op jit(solution)/shard_map/ppermute | solution.py:49
  14.3 27.7 %collective-permute-start.1 = (bf16[160,960]{1,0:T(8,128)(2,1)S(1)}, bf16[160,960]{1,0:T(8,128)(2,1)}, u32[]{:S(2)}, u32[]{:S(2)}) collective-permute-start(bf16[160,960]{1,0:T(8,128)(2,1)S(1)} %bitcast.233), channel_id=1, source_target_pairs={{0,16},{4,20},{8,24},{12,28},{16,0},{20,4},{24,8},{28,12},{1,17},{... | collective-permute-start | bytes 921608 | tf_op jit(solution)/shard_map/ppermute | solution.py:49
  15.4 29.3 %collective-permute-start.2 = (bf16[160,960]{1,0:T(8,128)(2,1)S(1)}, bf16[160,960]{1,0:T(8,128)(2,1)}, u32[]{:S(2)}, u32[]{:S(2)}) collective-permute-start(bf16[160,960]{1,0:T(8,128)(2,1)S(1)} %bitcast.234), channel_id=1, source_target_pairs={{0,24},{4,28},{8,0},{12,4},{16,8},{20,12},{24,16},{28,20},{1,25},{... | collective-permute-start | bytes 921608 | tf_op jit(solution)/shard_map/ppermute | solution.py:49
  44.7 12.2 %collective-permute-start.3 = (bf16[160,960]{1,0:T(8,128)(2,1)S(1)}, bf16[160,960]{1,0:T(8,128)(2,1)}, u32[]{:S(2)}, u32[]{:S(2)}) collective-permute-start(bf16[160,960]{1,0:T(8,128)(2,1)S(1)} %bitcast.235), channel_id=1, source_target_pairs={{0,4},{4,0},{8,12},{12,8},{16,20},{20,16},{24,28},{28,24},{1,5},{5... | collective-permute-start | bytes 921608 | tf_op jit(solution)/shard_map/ppermute | solution.py:61
  47.8 47.5 %all-to-all-start.1 = ((bf16[4,40,1792]{2,1,0:T(8,128)(2,1)}), bf16[4,40,1792]{2,1,0:T(8,128)(2,1)}, u32[]{:S(2)}, u32[]{:S(2)}) async-start(bf16[4,40,1792]{2,1,0:T(8,128)(2,1)} %pad_maximum_fusion.3), calls=%async_computation.1 | async-start | bytes 1146880 | tf_op jit(solution)/shard_map/all_to_all | solution.py:145
  53.5 41.8 %collective-permute-start.7 = (bf16[152,1280]{1,0:T(8,128)(2,1)}, bf16[152,1280]{1,0:T(8,128)(2,1)}, u32[]{:S(2)}, u32[]{:S(2)}) collective-permute-start(bf16[152,1280]{1,0:T(8,128)(2,1)} %pad_maximum_fusion.10), channel_id=1, source_target_pairs={{0,8},{4,12},{8,16},{12,20},{16,24},{20,28},{24,0},{28,4},{1,9},{5... | collective-permute-start | bytes 1167368 | tf_op jit(solution)/shard_map/ppermute | solution.py:49
  53.5 41.8 %collective-permute-start.8 = (bf16[152,1280]{1,0:T(8,128)(2,1)}, bf16[152,1280]{1,0:T(8,128)(2,1)}, u32[]{:S(2)}, u32[]{:S(2)}) collective-permute-start(bf16[152,1280]{1,0:T(8,128)(2,1)} %pad_maximum_fusion.10), channel_id=1, source_target_pairs={{0,16},{4,20},{8,24},{12,28},{16,0},{20,4},{24,8},{28,12},{1,17},{... | collective-permute-start | bytes 1167368 | tf_op jit(solution)/shard_map/ppermute | solution.py:49
  54.8 40.5 %collective-permute-start.9 = (bf16[152,1280]{1,0:T(8,128)(2,1)}, bf16[152,1280]{1,0:T(8,128)(2,1)}, u32[]{:S(2)}, u32[]{:S(2)}) collective-permute-start(bf16[152,1280]{1,0:T(8,128)(2,1)} %pad_maximum_fusion.10), channel_id=1, source_target_pairs={{0,24},{4,28},{8,0},{12,4},{16,8},{20,12},{24,16},{28,20},{1,25},{... | collective-permute-start | bytes 1167368 | tf_op jit(solution)/shard_map/ppermute | solution.py:49
  56.3 8.3 %collective-permute-start.4 = (bf16[160,960]{1,0:T(8,128)(2,1)}, bf16[160,960]{1,0:T(8,128)(2,1)S(1)}, u32[]{:S(2)}, u32[]{:S(2)}) collective-permute-start(bf16[160,960]{1,0:T(8,128)(2,1)} %collective-permute-done), channel_id=1, source_target_pairs={{0,4},{4,0},{8,12},{12,8},{16,20},{20,16},{24,28},{28,24},{1,5},{5... | collective-permute-start | bytes 921608 | tf_op jit(solution)/shard_map/ppermute | solution.py:61
  56.9 14.7 %collective-permute-start.5 = (bf16[160,960]{1,0:T(8,128)(2,1)}, bf16[160,960]{1,0:T(8,128)(2,1)S(1)}, u32[]{:S(2)}, u32[]{:S(2)}) collective-permute-start(bf16[160,960]{1,0:T(8,128)(2,1)} %collective-permute-done.1), channel_id=1, source_target_pairs={{0,4},{4,0},{8,12},{12,8},{16,20},{20,16},{24,28},{28,24},{1,5},{5... | collective-permute-start | bytes 921608 | tf_op jit(solution)/shard_map/ppermute | solution.py:61
  64.6 13.9 %collective-permute-start.6 = (bf16[160,960]{1,0:T(8,128)(2,1)}, bf16[160,960]{1,0:T(8,128)(2,1)S(1)}, u32[]{:S(2)}, u32[]{:S(2)}) collective-permute-start(bf16[160,960]{1,0:T(8,128)(2,1)} %collective-permute-done.2), channel_id=1, source_target_pairs={{0,4},{4,0},{8,12},{12,8},{16,20},{20,16},{24,28},{28,24},{1,5},{5... | collective-permute-start | bytes 921608 | tf_op jit(solution)/shard_map/ppermute | solution.py:61
  80.7 4.4 %copy-start.16 = (f32[1280]{0:T(1024)S(1)}, f32[1280]{0:T(1024)}, u32[]{:S(2)}) copy-start(f32[1280]{0:T(1024)} %param.13) | copy-start | bytes 15364
  85.2 2.4 copy-start.10
  87.5 15.1 %copy-start.3 = (bf16[2,512,5,64]{1,3,2,0:T(8,128)(2,1)}, bf16[2,512,5,64]{1,3,2,0:T(8,128)(2,1)S(1)}, u32[]{:S(2)}) copy-start(bf16[2,512,5,64]{1,3,2,0:T(8,128)(2,1)S(1)} %fusion.44) | copy-start | bytes 1966084
  95.3 5.6 %copy-start.8 = (f32[2,512,5,64]{1,3,2,0:T(8,128)S(1)}, f32[2,512,5,64]{1,3,2,0:T(8,128)}, u32[]{:S(2)}) copy-start(f32[2,512,5,64]{1,3,2,0:T(8,128)} %fusion.46) | copy-start | bytes 3932164
  95.3 56.7 %collective-permute-start.10 = (bf16[160,1792]{1,0:T(8,128)(2,1)}, bf16[160,1792]{1,0:T(8,128)(2,1)}, u32[]{:S(2)}, u32[]{:S(2)}) collective-permute-start(bf16[160,1792]{1,0:T(8,128)(2,1)} %bitcast.28), channel_id=1, source_target_pairs={{0,8},{4,12},{8,16},{12,20},{16,24},{20,28},{24,0},{28,4},{1,9},{5... | collective-permute-start | bytes 1720328 | tf_op jit(solution)/shard_map/ppermute | solution.py:49
  95.8 56.3 %collective-permute-start.11 = (bf16[160,1792]{1,0:T(8,128)(2,1)}, bf16[160,1792]{1,0:T(8,128)(2,1)}, u32[]{:S(2)}, u32[]{:S(2)}) collective-permute-start(bf16[160,1792]{1,0:T(8,128)(2,1)} %bitcast.28), channel_id=1, source_target_pairs={{0,16},{4,20},{8,24},{12,28},{16,0},{20,4},{24,8},{28,12},{1,17},{... | collective-permute-start | bytes 1720328 | tf_op jit(solution)/shard_map/ppermute | solution.py:49
  98.6 53.4 %collective-permute-start.12 = (bf16[160,1792]{1,0:T(8,128)(2,1)}, bf16[160,1792]{1,0:T(8,128)(2,1)}, u32[]{:S(2)}, u32[]{:S(2)}) collective-permute-start(bf16[160,1792]{1,0:T(8,128)(2,1)} %bitcast.28), channel_id=1, source_target_pairs={{0,24},{4,28},{8,0},{12,4},{16,8},{20,12},{24,16},{28,20},{1,25},{... | collective-permute-start | bytes 1720328 | tf_op jit(solution)/shard_map/ppermute | solution.py:49
  101.1 2.1 copy-start.11
  118.4 8.6 %collective-permute-start.13 = (bf16[152,1280]{1,0:T(8,128)(2,1)}, bf16[152,1280]{1,0:T(8,128)(2,1)S(1)}, u32[]{:S(2)}, u32[]{:S(2)}) collective-permute-start(bf16[152,1280]{1,0:T(8,128)(2,1)} %pad_maximum_fusion.10), channel_id=1, source_target_pairs={{0,4},{4,0},{8,12},{12,8},{16,20},{20,16},{24,28},{28,24},{1,5},{5... | collective-permute-start | bytes 1167368 | tf_op jit(solution)/shard_map/ppermute | solution.py:61
  118.7 16.6 %collective-permute-start.14 = (bf16[152,1280]{1,0:T(8,128)(2,1)}, bf16[152,1280]{1,0:T(8,128)(2,1)S(1)}, u32[]{:S(2)}, u32[]{:S(2)}) collective-permute-start(bf16[152,1280]{1,0:T(8,128)(2,1)} %collective-permute-done.7), channel_id=1, source_target_pairs={{0,4},{4,0},{8,12},{12,8},{16,20},{20,16},{24,28},{28,24},{1,5},{5... | collective-permute-start | bytes 1167368 | tf_op jit(solution)/shard_map/ppermute | solution.py:61
  127.0 16.7 %collective-permute-start.15 = (bf16[152,1280]{1,0:T(8,128)(2,1)}, bf16[152,1280]{1,0:T(8,128)(2,1)S(1)}, u32[]{:S(2)}, u32[]{:S(2)}) collective-permute-start(bf16[152,1280]{1,0:T(8,128)(2,1)} %collective-permute-done.8), channel_id=1, source_target_pairs={{0,4},{4,0},{8,12},{12,8},{16,20},{20,16},{24,28},{28,24},{1,5},{5... | collective-permute-start | bytes 1167368 | tf_op jit(solution)/shard_map/ppermute | solution.py:61
  135.3 16.7 %collective-permute-start.16 = (bf16[152,1280]{1,0:T(8,128)(2,1)}, bf16[152,1280]{1,0:T(8,128)(2,1)S(1)}, u32[]{:S(2)}, u32[]{:S(2)}) collective-permute-start(bf16[152,1280]{1,0:T(8,128)(2,1)} %collective-permute-done.9), channel_id=1, source_target_pairs={{0,4},{4,0},{8,12},{12,8},{16,20},{20,16},{24,28},{28,24},{1,5},{5... | collective-permute-start | bytes 1167368 | tf_op jit(solution)/shard_map/ppermute | solution.py:61
  152.1 15.7 %collective-permute-start.21 = (bf16[160,1792]{1,0:T(8,128)(2,1)}, bf16[160,1792]{1,0:T(8,128)(2,1)}, u32[]{:S(2)}, u32[]{:S(2)}) collective-permute-start(bf16[160,1792]{1,0:T(8,128)(2,1)} %bitcast.28), channel_id=1, source_target_pairs={{0,4},{4,0},{8,12},{12,8},{16,20},{20,16},{24,28},{28,24},{1,5},{5... | collective-permute-start | bytes 1720328 | tf_op jit(solution)/shard_map/ppermute | solution.py:61
  155.8 41.6 %all-to-all-start.2 = ((bf16[4,256,320]{1,2,0:T(8,128)(2,1)}), bf16[4,256,320]{1,2,0:T(8,128)(2,1)}, u32[]{:S(2)}, u32[]{:S(2)}) async-start(bf16[4,256,320]{1,2,0:T(8,128)(2,1)} %bitcast.221), calls=%async_computation.2 | async-start | bytes 1310720 | tf_op jit(solution)/shard_map/all_to_all | solution.py:216
  163.6 26.0 %collective-permute-start.17 = (bf16[8,40,1280]{2,1,0:T(8,128)(2,1)}, bf16[8,40,1280]{2,1,0:T(8,128)(2,1)S(1)}, u32[]{:S(2)}, u32[]{:S(2)}) collective-permute-start(bf16[8,40,1280]{2,1,0:T(8,128)(2,1)} %get-tuple-element.52), channel_id=1, source_target_pairs={{0,2},{1,3},{2,0},{3,1},{4,6},{5,7},{6,4},{7,5},{8,10},{9,11},{10,... | collective-permute-start | bytes 2457608 | tf_op jit(solution)/shard_map/ppermute | solution.py:41
  163.7 27.9 %collective-permute-start.22 = (bf16[160,1792]{1,0:T(8,128)(2,1)}, bf16[160,1792]{1,0:T(8,128)(2,1)S(1)}, u32[]{:S(2)}, u32[]{:S(2)}) collective-permute-start(bf16[160,1792]{1,0:T(8,128)(2,1)} %collective-permute-done.10), channel_id=1, source_target_pairs={{0,4},{4,0},{8,12},{12,8},{16,20},{20,16},{24,28},{28,24},{1,5},{5... | collective-permute-start | bytes 1720328 | tf_op jit(solution)/shard_map/ppermute | solution.py:61
  164.9 37.9 %collective-permute-start.23 = (bf16[160,1792]{1,0:T(8,128)(2,1)}, bf16[160,1792]{1,0:T(8,128)(2,1)}, u32[]{:S(2)}, u32[]{:S(2)}) collective-permute-start(bf16[160,1792]{1,0:T(8,128)(2,1)} %collective-permute-done.11), channel_id=1, source_target_pairs={{0,4},{4,0},{8,12},{12,8},{16,20},{20,16},{24,28},{28,24},{1,5},{5... | collective-permute-start | bytes 1720328 | tf_op jit(solution)/shard_map/ppermute | solution.py:61
  165.2 54.8 %collective-permute-start.24 = (bf16[160,1792]{1,0:T(8,128)(2,1)}, bf16[160,1792]{1,0:T(8,128)(2,1)}, u32[]{:S(2)}, u32[]{:S(2)}) collective-permute-start(bf16[160,1792]{1,0:T(8,128)(2,1)} %collective-permute-done.12), channel_id=1, source_target_pairs={{0,4},{4,0},{8,12},{12,8},{16,20},{20,16},{24,28},{28,24},{1,5},{5... | collective-permute-start | bytes 1720328 | tf_op jit(solution)/shard_map/ppermute | solution.py:61
  189.9 3.7 %collective-permute-start.18 = (bf16[2,8,40,1280]{3,2,1,0:T(8,128)(2,1)S(1)}, bf16[2,8,40,1280]{3,2,1,0:T(8,128)(2,1)S(1)}, u32[]{:S(2)}, u32[]{:S(2)}) collective-permute-start(bf16[2,8,40,1280]{3,2,1,0:T(8,128)(2,1)S(1)} %maximum_select_fusion.3), channel_id=1, source_target_pairs={{0,1},{1,0},{2,3},{3,2},{4,5},{5,4},{6,7},{7,6},{8,9},{9,8},{10,11... | collective-permute-start | bytes 4915208 | tf_op jit(solution)/shard_map/ppermute | solution.py:41
  192.7 2.1 copy-start.1
  195.4 7.5 %slice-start = ((s8[4587520]{0:T(1024)(128)(4,1)}), s8[393216]{0:T(1024)(128)(4,1)S(1)}, s32[]{:S(2)}) async-start(s8[4587520]{0:T(1024)(128)(4,1)} %bitcast.206), calls=%async_computation.3 | async-start | bytes 786432
  197.4 3.8 %copy-start.14 = (f32[1280]{0:T(1024)S(1)}, f32[1280]{0:T(1024)}, u32[]{:S(2)}) copy-start(f32[1280]{0:T(1024)} %param.14) | copy-start | bytes 15364
  197.4 5.4 %slice-start.1 = ((s8[4587520]{0:T(1024)(128)(4,1)}), s8[4194304]{0:T(1024)(128)(4,1)S(1)}, s32[]{:S(2)}) async-start(s8[4587520]{0:T(1024)(128)(4,1)} %bitcast.206), calls=%async_computation.4 | async-start | bytes 8388608
  201.4 16.4 %collective-permute-start.19 = (bf16[256,1280]{1,0:T(8,128)(2,1)S(1)}, bf16[256,1280]{1,0:T(8,128)(2,1)S(1)}, u32[]{:S(2)}, u32[]{:S(2)}) collective-permute-start(bf16[256,1280]{1,0:T(8,128)(2,1)S(1)} %multiply_convert_fusion.3), channel_id=1, source_target_pairs={{0,2},{1,3},{2,0},{3,1},{4,6},{5,7},{6,4},{7,5},{8,10},{9,11},{10,... | collective-permute-start | bytes 1966088 | tf_op jit(solution)/shard_map/ppermute | solution.py:41
  218.0 3.5 %collective-permute-start.20 = (bf16[2,256,1280]{2,1,0:T(8,128)(2,1)S(1)}, bf16[2,256,1280]{2,1,0:T(8,128)(2,1)S(1)}, u32[]{:S(2)}, u32[]{:S(2)}) collective-permute-start(bf16[2,256,1280]{2,1,0:T(8,128)(2,1)S(1)} %maximum_select_fusion.5), channel_id=1, source_target_pairs={{0,1},{1,0},{2,3},{3,2},{4,5},{5,4},{6,7},{7,6},{8,9},{9,8},{10,11... | collective-permute-start | bytes 3932168 | tf_op jit(solution)/shard_map/ppermute | solution.py:41
  221.1 2.6 copy-start.2
  223.7 2.8 copy-start.7
  235.0 14.2 %collective-permute-start.25 = (bf16[2,128,1280]{2,1,0:T(8,128)(2,1)S(1)}, bf16[2,128,1280]{2,1,0:T(8,128)(2,1)S(1)}, u32[]{:S(2)}, u32[]{:S(2)}) collective-permute-start(bf16[2,128,1280]{2,1,0:T(8,128)(2,1)S(1)} %dynamic-slice_bitcast_fusion.1), channel_id=1, source_target_pairs={{0,1},{1,0},{2,3},{3,2},{4,5},{5,4},{6,7},{7,6},{8,9},{9,8},{10,11... | collective-permute-start | bytes 1966088 | tf_op jit(solution)/shard_map/ppermute | solution.py:41
  247.7 4.3 %copy-start.9 = (bf16[512,1280]{1,0:T(8,128)(2,1)S(1)}, bf16[512,1280]{1,0:T(8,128)(2,1)}, u32[]{:S(2)}) copy-start(bf16[512,1280]{1,0:T(8,128)(2,1)} %convolution_convert_fusion) | copy-start | bytes 3932164
  248.9 3.0 %collective-permute-start.29 = (bf16[2,128,1280]{2,1,0:T(8,128)(2,1)S(1)}, bf16[2,128,1280]{2,1,0:T(8,128)(2,1)S(1)}, u32[]{:S(2)}, u32[]{:S(2)}) collective-permute-start(bf16[2,128,1280]{2,1,0:T(8,128)(2,1)S(1)} %dynamic-slice_bitcast_fusion), channel_id=1, source_target_pairs={{0,1},{1,0},{2,3},{3,2},{4,5},{5,4},{6,7},{7,6},{8,9},{9,8},{10,11... | collective-permute-start | bytes 1966088 | tf_op jit(solution)/shard_map/ppermute | solution.py:41
  250.4 1.5 copy-start.5
  250.5 9.1 %collective-permute-start.26 = (bf16[128,1280]{1,0:T(8,128)(2,1)S(1)}, bf16[128,1280]{1,0:T(8,128)(2,1)S(1)}, u32[]{:S(2)}, u32[]{:S(2)}) collective-permute-start(bf16[128,1280]{1,0:T(8,128)(2,1)S(1)} %fusion.42), channel_id=1, source_target_pairs={{0,2},{1,3},{2,0},{3,1},{4,6},{5,7},{6,4},{7,5},{8,10},{9,11},{10,... | collective-permute-start | bytes 983048 | tf_op jit(solution)/shard_map/ppermute | solution.py:41
  252.1 1.1 copy-start.6
  253.1 16.6 %copy-start.4 = (bf16[2,512,5,64]{1,3,2,0:T(8,128)(2,1)S(1)}, bf16[2,512,5,64]{1,3,2,0:T(8,128)(2,1)}, u32[]{:S(2)}) copy-start(bf16[2,512,5,64]{1,3,2,0:T(8,128)(2,1)} %copy-done.3) | copy-start | bytes 1966084
  253.9 12.7 %collective-permute-start.30 = (bf16[128,1280]{1,0:T(8,128)(2,1)}, bf16[128,1280]{1,0:T(8,128)(2,1)}, u32[]{:S(2)}, u32[]{:S(2)}) collective-permute-start(bf16[128,1280]{1,0:T(8,128)(2,1)} %fusion.43), channel_id=1, source_target_pairs={{0,2},{1,3},{2,0},{3,1},{4,6},{5,7},{6,4},{7,5},{8,10},{9,11},{10,... | collective-permute-start | bytes 983048 | tf_op jit(solution)/shard_map/ppermute | solution.py:41
  259.5 0.7 copy-start.12
  268.3 8.2 %collective-permute-start.31 = (bf16[128,1280]{1,0:T(8,128)(2,1)S(1)}, bf16[128,1280]{1,0:T(8,128)(2,1)}, u32[]{:S(2)}, u32[]{:S(2)}) collective-permute-start(bf16[128,1280]{1,0:T(8,128)(2,1)S(1)} %get-tuple-element.63), channel_id=1, source_target_pairs={{0,2},{1,3},{2,0},{3,1},{4,6},{5,7},{6,4},{7,5},{8,10},{9,11},{10,... | collective-permute-start | bytes 983048 | tf_op jit(solution)/shard_map/ppermute | solution.py:41
  270.5 13.0 %collective-permute-start.27 = (bf16[128,1280]{1,0:T(8,128)(2,1)S(1)}, bf16[128,1280]{1,0:T(8,128)(2,1)S(1)}, u32[]{:S(2)}, u32[]{:S(2)}) collective-permute-start(bf16[128,1280]{1,0:T(8,128)(2,1)S(1)} %get-tuple-element.62), channel_id=1, source_target_pairs={{0,2},{1,3},{2,0},{3,1},{4,6},{5,7},{6,4},{7,5},{8,10},{9,11},{10,... | collective-permute-start | bytes 983048 | tf_op jit(solution)/shard_map/ppermute | solution.py:41
  277.7 9.3 %collective-permute-start.32 = (bf16[2,128,1280]{2,1,0:T(8,128)(2,1)S(1)}, bf16[2,128,1280]{2,1,0:T(8,128)(2,1)S(1)}, u32[]{:S(2)}, u32[]{:S(2)}) collective-permute-start(bf16[2,128,1280]{2,1,0:T(8,128)(2,1)S(1)} %maximum_select_fusion.10), channel_id=1, source_target_pairs={{0,1},{1,0},{2,3},{3,2},{4,5},{5,4},{6,7},{7,6},{8,9},{9,8},{10,11... | collective-permute-start | bytes 1966088 | tf_op jit(solution)/shard_map/ppermute | solution.py:41
  283.6 3.9 %collective-permute-start.28 = (bf16[2,128,1280]{2,1,0:T(8,128)(2,1)S(1)}, bf16[2,128,1280]{2,1,0:T(8,128)(2,1)S(1)}, u32[]{:S(2)}, u32[]{:S(2)}) collective-permute-start(bf16[2,128,1280]{2,1,0:T(8,128)(2,1)S(1)} %maximum_select_fusion.8), channel_id=1, source_target_pairs={{0,1},{1,0},{2,3},{3,2},{4,5},{5,4},{6,7},{7,6},{8,9},{9,8},{10,11... | collective-permute-start | bytes 1966088 | tf_op jit(solution)/shard_map/ppermute | solution.py:41

commit v4 on v3

--- a/solution.py
+++ b/solution.py
@@ -50,7 +50,12 @@
     return held
 
 
-def gather_near(held):
+def swap_near(held):
+    count = lax.axis_size("req")
+    return [lax.ppermute(mine, "req", [(r, r ^ 1) for r in range(count)]) for mine in held]
+
+
+def gather_near(held, swapped):
     count = lax.axis_size("req")
     outer = len(held)
     shape = held[0].shape
@@ -58,7 +63,6 @@
     far, near = me // 2, me % 2
     out = jnp.zeros((outer, 2) + shape, held[0].dtype)
     zeros = (0,) * len(shape)
-    swapped = [lax.ppermute(mine, "req", [(r, r ^ 1) for r in range(count)]) for mine in held]
     for step, (mine, other) in enumerate(zip(held, swapped)):
         place = (far + outer - step) % outer
         out = lax.dynamic_update_slice(out, mine[None, None], (place, near) + zeros)
@@ -131,7 +135,7 @@
     third_pack = jnp.concatenate([o_master, down_master]).astype(half)
     first_far, third_pack = tie(first_far, third_pack)
     third_far = gather_far(third_pack)
-    first_full = gather_near(first_far).reshape(-1, q_cols + 2 * kv_cols)
+    first_full = gather_near(first_far, swap_near(first_far)).reshape(-1, q_cols + 2 * kv_cols)
 
     def ff_parts(master):
         return (
@@ -164,7 +168,7 @@
         queries, key_rows, value_rows, third_far, second_pack
     )
     second_far = gather_far(second_pack)
-    third_full = gather_near(third_far)
+    third_swapped = swap_near(third_far)
     cosine_table, sine_table = rope_tables(sequence_length, HEAD_DIM)
     q_rot = rotate(queries, cosine_table, sine_table).astype(jnp.bfloat16)
     rotated_keys = rotate(key_rows, cosine_table, sine_table).astype(jnp.bfloat16)
@@ -188,6 +192,9 @@
     v_local = jnp.einsum(
         "pshd,gh->psgd", value_halves, selector_mask, preferred_element_type=jnp.float32
     ).astype(jnp.bfloat16)
+    ahead = len(third_swapped) // 2
+    v_local, early = tie(v_local, third_swapped[:ahead])
+    third_full = gather_near(third_far, early + third_swapped[ahead:])
     scores = jnp.einsum(
         "pqhd,pkhd->phqk", q_rot, k_local, preferred_element_type=jnp.float32
     ) / math.sqrt(HEAD_DIM)
@@ -206,7 +213,7 @@
         .reshape(tok_rows, local_heads * HEAD_DIM)
     )
     attended, second_far, third_full = tie(attended, second_far, third_full)
-    second_full = gather_near(second_far).reshape(-1, 2 * ff_cols)
+    second_full = gather_near(second_far, swap_near(second_far)).reshape(-1, 2 * ff_cols)
     o_own, down_weight = third_full[:, :shard_rows], third_full[:, shard_rows:]
     down_weight = down_weight.reshape(ff_cols, model_width)
     o_full = gather_tp(o_own).transpose(1, 0, 2, 3).reshape(-1, model_width)

time: 294 us -> 286 us (0.973)
  waiting for transfers between devices: 109 us -> 104 us
    ppermute x12, waiting for transfers between devices: 43.1 us -> 27.7 us  [swap_near(): lax.ppermute(mine, 'req', [(r, r ^ 1) for r in range(count)])]
    ppermute x9, waiting for transfers between devices: 13.2 us -> 24.2 us  [gather_far(): held.append(lax.ppermute(shard, 'req', pairs))]
  transfers between devices with their start and end apart: 36 -> 36, of which waited for: 17 -> 18; matrix products, arithmetic and copies ran while one was open for 37% -> 38% of each run, Pallas kernels for 0% -> 0%
where the time goes in v4:
time: 286 us; the launch traced here: 283 us
  waiting for transfers between devices  104 us (36%)
  matrix products  50.8 us (18%)
  local copies, waits for them, and re-layouts  48.4 us (17%)
  starting transfers between devices  47.3 us (17%)
  other arithmetic  31.2 us (11%)
    ppermute x12, waiting for transfers between devices, tp_permute(): lax.ppermute(field, 'tp', [(s, s ^ flip) for s in range(lax.axis_size('tp...  52.5 us
    ppermute x12, waiting for transfers between devices, swap_near(): lax.ppermute(mine, 'req', [(r, r ^ 1) for r in range(count)])  27.7 us
    ppermute x9, waiting for transfers between devices, gather_far(): held.append(lax.ppermute(shard, 'req', pairs))  24.2 us
    dot_general x2, matrix products, local(): jnp.dot(hidden_ff, down_weight, preferred_element_type=jnp.float32)  14.8 us
    ppermute x12, starting transfers between devices, tp_permute(): lax.ppermute(field, 'tp', [(s, s ^ flip) for s in range(lax.axis_size('tp...  13.5 us
    dynamic_update_slice x12, local copies, waits for them, and re-layouts, gather_near(): out = lax.dynamic_update_slice(out, mine[None, None], (place, near) + zeros)  11.6 us
    ppermute x9, starting transfers between devices, gather_far(): held.append(lax.ppermute(shard, 'req', pairs))  9.93 us
    sub x1, matrix products, local(): expo = jnp.exp(scores - highest)  9.51 us
  transfers between devices with their start and end apart: 36, of which 18 were waited for; matrix products, arithmetic and copies ran while one was open for 38% of the time, Pallas kernels for 0%

profile of v4, /device:TPU:13, one launch (start us, length us, event | category | flops | bytes accessed | tf_op | source)
XLA Modules:
  0.0 283.4 jit_solution(10154356370008090445)
XLA Ops:
  3.8 4.2 %all-to-all-start = ((bf16[4,40,960]{2,1,0:T(8,128)(2,1)}), bf16[4,40,960]{2,1,0:T(8,128)(2,1)S(1)}, u32[]{:S(2)}, u32[]{:S(2)}) async-start(bf16[4,40,960]{2,1,0:T(8,128)(2,1)} %pad_maximum_fusion.11), calls=%async_computation | async-start | bytes 655360 | tf_op jit(solution)/shard_map/all_to_all | solution.py:130
  10.0 2.7 convert.37
  13.0 1.3 collective-permute-start
  15.4 1.4 collective-permute-start.2
  16.8 1.8 convert.27
  18.7 1.8 convert_element_type.123
  20.5 1.4 reshape.498
  22.6 2.0 concatenate.94
  24.6 1.8 convert_element_type.122
  26.4 1.4 reshape.497
  28.6 1.3 concatenate.93
  29.8 1.7 pad_maximum_fusion.10
  31.6 10.5 %collective-permute-done.1 = bf16[160,960]{1,0:T(8,128)(2,1)} collective-permute-done((bf16[160,960]{1,0:T(8,128)(2,1)S(1)}, bf16[160,960]{1,0:T(8,128)(2,1)}, u32[]{:S(2)}, u32[]{:S(2)}) %collective-permute-start.1) | collective-permute-done | bytes 307232 | tf_op jit(solution)/shard_map/ppermute | solution.py:49
  42.1 2.7 collective-permute-done.2
  46.0 1.8 pad_maximum_fusion.3
  47.8 5.7 %all-to-all-start.1 = ((bf16[4,40,1792]{2,1,0:T(8,128)(2,1)}), bf16[4,40,1792]{2,1,0:T(8,128)(2,1)}, u32[]{:S(2)}, u32[]{:S(2)}) async-start(bf16[4,40,1792]{2,1,0:T(8,128)(2,1)} %pad_maximum_fusion.3), calls=%async_computation.1 | async-start | bytes 1146880 | tf_op jit(solution)/shard_map/all_to_all | solution.py:149
  53.5 1.3 collective-permute-start.8
  54.8 1.5 collective-permute-start.9
  56.9 1.3 collective-permute-start.5
  60.2 4.4 %collective-permute-done.4 = bf16[160,960]{1,0:T(8,128)(2,1)S(1)} collective-permute-done((bf16[160,960]{1,0:T(8,128)(2,1)}, bf16[160,960]{1,0:T(8,128)(2,1)S(1)}, u32[]{:S(2)}, u32[]{:S(2)}) %collective-permute-start.4) | collective-permute-done | bytes 307232 | tf_op jit(solution)/shard_map/ppermute | solution.py:55
  65.9 5.7 %collective-permute-done.5 = bf16[160,960]{1,0:T(8,128)(2,1)S(1)} collective-permute-done((bf16[160,960]{1,0:T(8,128)(2,1)}, bf16[160,960]{1,0:T(8,128)(2,1)S(1)}, u32[]{:S(2)}, u32[]{:S(2)}) %collective-permute-start.5) | collective-permute-done | bytes 307232 | tf_op jit(solution)/shard_map/ppermute | solution.py:55
  72.7 5.9 %collective-permute-done.6 = bf16[160,960]{1,0:T(8,128)(2,1)S(1)} collective-permute-done((bf16[160,960]{1,0:T(8,128)(2,1)}, bf16[160,960]{1,0:T(8,128)(2,1)S(1)}, u32[]{:S(2)}, u32[]{:S(2)}) %collective-permute-start.6) | collective-permute-done | bytes 307232 | tf_op jit(solution)/shard_map/ppermute | solution.py:55
  78.6 2.2 slice_bitcast_fusion
  80.7 2.2 copy.50
  82.9 2.2 copy.52
  85.2 2.3 fusion.44
  87.5 2.2 fusion.48
  89.7 2.2 copy.51
  91.9 3.3 %fusion.46 = f32[2,512,5,64]{1,3,2,0:T(8,128)} fusion(bf16[5,64,1280,1]{2,1,0,3:T(8,128)(2,1)} %bitcast.246, bf16[2,512,1280]{2,1,0:T(8,128)(2,1)S(1)} %copy-done, f32[1280]{0:T(1024)S(1)} %copy-done.16, f32[2,512]{1,0:T(2,128)S(1)} %add_rsqrt_fusion), kind=kOutput, calls=%fused_computation.114 | convolution fusion | flops 844103680 | bytes 4760576 | tf_op jit(solution)/shard_map/dot_general | solution.py:161
  95.8 2.9 %collective-permute-start.13 = (bf16[160,1792]{1,0:T(8,128)(2,1)}, bf16[160,1792]{1,0:T(8,128)(2,1)}, u32[]{:S(2)}, u32[]{:S(2)}) collective-permute-start(bf16[160,1792]{1,0:T(8,128)(2,1)} %bitcast.28), channel_id=1, source_target_pairs={{0,16},{4,20},{8,24},{12,28},{16,0},{20,4},{24,8},{28,12},{1,17},{... | collective-permute-start | bytes 1720328 | tf_op jit(solution)/shard_map/ppermute | solution.py:49
  98.6 2.3 subtract_convert_fusion
  101.2 1.5 fusion.20
  103.7 1.2 collective-permute-start.11
  104.9 9.5 %fusion.66 = (f32[2,5,512]{2,1,0:T(8,128)S(1)}, f32[2,5,512,512]{2,3,1,0:T(8,128)}) fusion(pred[2,512,512]{1,2,0:T(8,128)(4,1)S(1)} %copy-done.11, bf16[2,512,5,32]{1,3,2,0:T(8,128)(2,1)} %get-tuple-element.67, bf16[2,512,5,32]{1,3,2,0:T(8,128)(2,1)} %get-tuple-element.66, bf16[2,512,5,64]{1,2,3,0:T(8,128)(2,1)} %fusion.20), kind=kOutput, calls=%fused_computation.141 | convolution fusion | flops 347341312 | bytes 12341248 | tf_op jit(solution)/shard_map/sub | solution.py:208
  115.9 4.4 %collective-permute-done.11 = bf16[152,1280]{1,0:T(8,128)(2,1)S(1)} collective-permute-done((bf16[152,1280]{1,0:T(8,128)(2,1)}, bf16[152,1280]{1,0:T(8,128)(2,1)S(1)}, u32[]{:S(2)}, u32[]{:S(2)}) %collective-permute-start.11) | collective-permute-done | bytes 389152 | tf_op jit(solution)/shard_map/ppermute | solution.py:55
  121.6 5.0 %fusion.22 = bf16[2,512,5,64]{1,3,2,0:T(8,128)(2,1)S(1)} fusion(f32[2,5,512,512]{2,3,1,0:T(8,128)} %get-tuple-element.73, f32[2,5,512]{2,1,0:T(8,128)S(1)} %get-tuple-element.72, bf16[2,512,5,64]{1,2,3,0:T(8,128)(2,1)S(1)} %fusion.19), kind=kOutput, calls=%fused_computation.45 | convolution fusion | flops 341114880 | bytes 11816960 | tf_op jit(solution)/shard_map/phqk,pkhd->pqhd/dot_general | solution.py:211
  130.4 6.5 %collective-permute-done.16 = bf16[152,1280]{1,0:T(8,128)(2,1)S(1)} collective-permute-done((bf16[152,1280]{1,0:T(8,128)(2,1)}, bf16[152,1280]{1,0:T(8,128)(2,1)S(1)}, u32[]{:S(2)}, u32[]{:S(2)}) %collective-permute-start.16) | collective-permute-done | bytes 389152 | tf_op jit(solution)/shard_map/ppermute | solution.py:55
  136.9 6.6 %collective-permute-done.13 = bf16[160,1792]{1,0:T(8,128)(2,1)} collective-permute-done((bf16[160,1792]{1,0:T(8,128)(2,1)}, bf16[160,1792]{1,0:T(8,128)(2,1)}, u32[]{:S(2)}, u32[]{:S(2)}) %collective-permute-start.13) | collective-permute-done | bytes 573472 | tf_op jit(solution)/shard_map/ppermute | solution.py:49
  143.5 4.5 %collective-permute-done.14 = bf16[160,1792]{1,0:T(8,128)(2,1)} collective-permute-done((bf16[160,1792]{1,0:T(8,128)(2,1)}, bf16[160,1792]{1,0:T(8,128)(2,1)}, u32[]{:S(2)}, u32[]{:S(2)}) %collective-permute-start.14) | collective-permute-done | bytes 573472 | tf_op jit(solution)/shard_map/ppermute | solution.py:49
  149.3 1.5 slice.57
  151.7 5.9 %all-to-all-start.2 = ((bf16[4,256,320]{1,2,0:T(8,128)(2,1)}), bf16[4,256,320]{1,2,0:T(8,128)(2,1)}, u32[]{:S(2)}, u32[]{:S(2)}) async-start(bf16[4,256,320]{1,2,0:T(8,128)(2,1)} %bitcast.193), calls=%async_computation.2 | async-start | bytes 1310720 | tf_op jit(solution)/shard_map/all_to_all | solution.py:223
  162.9 20.7 %collective-permute-done.17 = bf16[8,40,1280]{2,1,0:T(8,128)(2,1)S(1)} collective-permute-done((bf16[8,40,1280]{2,1,0:T(8,128)(2,1)}, bf16[8,40,1280]{2,1,0:T(8,128)(2,1)S(1)}, u32[]{:S(2)}, u32[]{:S(2)}) %collective-permute-start.17) | collective-permute-done | bytes 819232 | tf_op jit(solution)/shard_map/ppermute | solution.py:41
  187.6 1.2 copy-done.1
  189.4 2.0 copy.62
  191.4 3.8 %multiply_reduce_fusion.1 = (f32[256]{0:T(256)S(1)}, f32[256,1280]{1,0:T(8,128)S(1)}) fusion(bf16[256,1280]{0,1:T(8,128)(2,1)} %bitcast.43, bf16[1280,1280]{1,0:T(8,128)(2,1)} %bitcast.196, f32[1024,1280]{1,0:T(8,128)} %convert.37, s32[]{:T(128)S(6)} %select_n.283), kind=kOutput, calls=%fused_computation.44 | convolution fusion | flops 839843584 | bytes 6554628 | tf_op jit(solution)/shard_map/dot_general | solution.py:225
  195.3 1.5 collective-permute-start.19
  198.1 13.6 %collective-permute-done.19 = bf16[256,1280]{1,0:T(8,128)(2,1)S(1)} collective-permute-done((bf16[256,1280]{1,0:T(8,128)(2,1)S(1)}, bf16[256,1280]{1,0:T(8,128)(2,1)S(1)}, u32[]{:S(2)}, u32[]{:S(2)}) %collective-permute-start.19) | collective-permute-done | bytes 655392 | tf_op jit(solution)/shard_map/ppermute | solution.py:41
  216.4 1.3 fusion.65
  217.6 2.8 fusion.13
  220.4 7.4 %convolution_convert_fusion.1 = bf16[512,1280]{1,0:T(8,128)(2,1)} fusion(bf16[896,1280]{1,0:T(8,128)(2,1)} %bitcast.224, f32[512,896]{1,0:T(8,128)} %fusion.13, bf16[512,1280]{1,0:T(8,128)(2,1)} %bitcast.230, bf16[1280,1792]{1,0:T(8,128)(2,1)} %bitcast.209), kind=kOutput, calls=%fused_computation.13 | convolution fusion | flops 2352218112 | bytes 9043968 | tf_op jit(solution)/shard_map/dot_general | solution.py:235
  229.4 4.8 %fusion.11 = f32[512,896]{1,0:T(8,128)} fusion(bf16[512,1280]{1,0:T(8,128)(2,1)} %bitcast.227, bf16[1280,1792]{1,0:T(8,128)(2,1)} %bitcast.210), kind=kOutput, calls=%fused_computation.22 | convolution fusion | flops 1174405120 | bytes 5439488 | tf_op jit(solution)/shard_map/dot_general | solution.py:231
  234.2 7.4 %convolution_convert_fusion = bf16[512,1280]{1,0:T(8,128)(2,1)} fusion(bf16[896,1280]{1,0:T(8,128)(2,1)} %bitcast.225, f32[512,896]{1,0:T(8,128)} %fusion.11, bf16[512,1280]{1,0:T(8,128)(2,1)} %bitcast.228, bf16[1280,1792]{1,0:T(8,128)(2,1)} %bitcast.211), kind=kOutput, calls=%fused_computation.12 | convolution fusion | flops 2352218112 | bytes 9043968 | tf_op jit(solution)/shard_map/dot_general | solution.py:235
  241.6 1.2 dynamic-slice_bitcast_fusion
  244.4 1.5 collective-permute-start.26
  248.8 4.7 %collective-permute-done.26 = bf16[128,1280]{1,0:T(8,128)(2,1)S(1)} collective-permute-done((bf16[128,1280]{1,0:T(8,128)(2,1)S(1)}, bf16[128,1280]{1,0:T(8,128)(2,1)S(1)}, u32[]{:S(2)}, u32[]{:S(2)}) %collective-permute-start.26) | collective-permute-done | bytes 327712 | tf_op jit(solution)/shard_map/ppermute | solution.py:41
  254.2 6.4 %collective-permute-done.30 = bf16[128,1280]{1,0:T(8,128)(2,1)} collective-permute-done((bf16[128,1280]{1,0:T(8,128)(2,1)}, bf16[128,1280]{1,0:T(8,128)(2,1)}, u32[]{:S(2)}, u32[]{:S(2)}) %collective-permute-start.30) | collective-permute-done | bytes 327712 | tf_op jit(solution)/shard_map/ppermute | solution.py:41
  260.6 1.7 fusion.34
  262.3 1.5 collective-permute-start.31
  264.6 1.5 pad_maximum_fusion.1
  266.1 4.4 %collective-permute-done.31 = bf16[128,1280]{1,0:T(8,128)(2,1)} collective-permute-done((bf16[128,1280]{1,0:T(8,128)(2,1)S(1)}, bf16[128,1280]{1,0:T(8,128)(2,1)}, u32[]{:S(2)}, u32[]{:S(2)}) %collective-permute-start.31) | collective-permute-done | bytes 327712 | tf_op jit(solution)/shard_map/ppermute | solution.py:41
  271.7 3.8 %collective-permute-start.32 = (bf16[2,128,1280]{2,1,0:T(8,128)(2,1)S(1)}, bf16[2,128,1280]{2,1,0:T(8,128)(2,1)S(1)}, u32[]{:S(2)}, u32[]{:S(2)}) collective-permute-start(bf16[2,128,1280]{2,1,0:T(8,128)(2,1)S(1)} %maximum_select_fusion.10), channel_id=1, source_target_pairs={{0,1},{1,0},{2,3},{3,2},{4,5},{5,4},{6,7},{7,6},{8,9},{9,8},{10,11... | collective-permute-start | bytes 1966088 | tf_op jit(solution)/shard_map/ppermute | solution.py:41
  275.5 1.9 collective-permute-done.27
  277.5 2.1 collective-permute-start.28
  281.7 1.7 pad_maximum_fusion
  (157 shorter events, 51.1 us)
Async XLA Ops:
  0.6 7.6 %copy-start.15 = (s32[2]{0:T(128)S(1)}, s32[2]{0:T(128)}, u32[]{:S(2)}) copy-start(s32[2]{0:T(128)} %param.12) | copy-start | bytes 28
  0.6 7.6 %copy-start = (bf16[2,512,1280]{2,1,0:T(8,128)(2,1)S(1)}, bf16[2,512,1280]{2,1,0:T(8,128)(2,1)}, u32[]{:S(2)}) copy-start(bf16[2,512,1280]{2,1,0:T(8,128)(2,1)} %param.11) | copy-start | bytes 7864324
  3.8 9.2 %all-to-all-start = ((bf16[4,40,960]{2,1,0:T(8,128)(2,1)}), bf16[4,40,960]{2,1,0:T(8,128)(2,1)S(1)}, u32[]{:S(2)}, u32[]{:S(2)}) async-start(bf16[4,40,960]{2,1,0:T(8,128)(2,1)} %pad_maximum_fusion.11), calls=%async_computation | async-start | bytes 655360 | tf_op jit(solution)/shard_map/all_to_all | solution.py:130
  10.0 8.6 %copy-start.13 = (f32[40,1280]{1,0:T(8,128)S(1)}, f32[40,1280]{1,0:T(8,128)}, u32[]{:S(2)}) copy-start(f32[40,1280]{1,0:T(8,128)} %param.18) | copy-start | bytes 614404
  13.0 18.6 %collective-permute-start = (bf16[160,960]{1,0:T(8,128)(2,1)S(1)}, bf16[160,960]{1,0:T(8,128)(2,1)}, u32[]{:S(2)}, u32[]{:S(2)}) collective-permute-start(bf16[160,960]{1,0:T(8,128)(2,1)S(1)} %bitcast.231), channel_id=1, source_target_pairs={{0,8},{4,12},{8,16},{12,20},{16,24},{20,28},{24,0},{28,4},{1,9},{5... | collective-permute-start | bytes 921608 | tf_op jit(solution)/shard_map/ppermute | solution.py:49
  14.3 27.7 %collective-permute-start.1 = (bf16[160,960]{1,0:T(8,128)(2,1)S(1)}, bf16[160,960]{1,0:T(8,128)(2,1)}, u32[]{:S(2)}, u32[]{:S(2)}) collective-permute-start(bf16[160,960]{1,0:T(8,128)(2,1)S(1)} %bitcast.232), channel_id=1, source_target_pairs={{0,16},{4,20},{8,24},{12,28},{16,0},{20,4},{24,8},{28,12},{1,17},{... | collective-permute-start | bytes 921608 | tf_op jit(solution)/shard_map/ppermute | solution.py:49
  15.4 29.3 %collective-permute-start.2 = (bf16[160,960]{1,0:T(8,128)(2,1)S(1)}, bf16[160,960]{1,0:T(8,128)(2,1)}, u32[]{:S(2)}, u32[]{:S(2)}) collective-permute-start(bf16[160,960]{1,0:T(8,128)(2,1)S(1)} %bitcast.233), channel_id=1, source_target_pairs={{0,24},{4,28},{8,0},{12,4},{16,8},{20,12},{24,16},{28,20},{1,25},{... | collective-permute-start | bytes 921608 | tf_op jit(solution)/shard_map/ppermute | solution.py:49
  44.7 12.2 %collective-permute-start.3 = (bf16[160,960]{1,0:T(8,128)(2,1)S(1)}, bf16[160,960]{1,0:T(8,128)(2,1)}, u32[]{:S(2)}, u32[]{:S(2)}) collective-permute-start(bf16[160,960]{1,0:T(8,128)(2,1)S(1)} %bitcast.234), channel_id=1, source_target_pairs={{0,4},{4,0},{8,12},{12,8},{16,20},{20,16},{24,28},{28,24},{1,5},{5... | collective-permute-start | bytes 921608 | tf_op jit(solution)/shard_map/ppermute | solution.py:55
  47.8 47.5 %all-to-all-start.1 = ((bf16[4,40,1792]{2,1,0:T(8,128)(2,1)}), bf16[4,40,1792]{2,1,0:T(8,128)(2,1)}, u32[]{:S(2)}, u32[]{:S(2)}) async-start(bf16[4,40,1792]{2,1,0:T(8,128)(2,1)} %pad_maximum_fusion.3), calls=%async_computation.1 | async-start | bytes 1146880 | tf_op jit(solution)/shard_map/all_to_all | solution.py:149
  53.5 41.8 %collective-permute-start.7 = (bf16[152,1280]{1,0:T(8,128)(2,1)}, bf16[152,1280]{1,0:T(8,128)(2,1)}, u32[]{:S(2)}, u32[]{:S(2)}) collective-permute-start(bf16[152,1280]{1,0:T(8,128)(2,1)} %pad_maximum_fusion.10), channel_id=1, source_target_pairs={{0,8},{4,12},{8,16},{12,20},{16,24},{20,28},{24,0},{28,4},{1,9},{5... | collective-permute-start | bytes 1167368 | tf_op jit(solution)/shard_map/ppermute | solution.py:49
  53.5 41.8 %collective-permute-start.8 = (bf16[152,1280]{1,0:T(8,128)(2,1)}, bf16[152,1280]{1,0:T(8,128)(2,1)}, u32[]{:S(2)}, u32[]{:S(2)}) collective-permute-start(bf16[152,1280]{1,0:T(8,128)(2,1)} %pad_maximum_fusion.10), channel_id=1, source_target_pairs={{0,16},{4,20},{8,24},{12,28},{16,0},{20,4},{24,8},{28,12},{1,17},{... | collective-permute-start | bytes 1167368 | tf_op jit(solution)/shard_map/ppermute | solution.py:49
  54.8 40.5 %collective-permute-start.9 = (bf16[152,1280]{1,0:T(8,128)(2,1)}, bf16[152,1280]{1,0:T(8,128)(2,1)}, u32[]{:S(2)}, u32[]{:S(2)}) collective-permute-start(bf16[152,1280]{1,0:T(8,128)(2,1)} %pad_maximum_fusion.10), channel_id=1, source_target_pairs={{0,24},{4,28},{8,0},{12,4},{16,8},{20,12},{24,16},{28,20},{1,25},{... | collective-permute-start | bytes 1167368 | tf_op jit(solution)/shard_map/ppermute | solution.py:49
  56.3 8.3 %collective-permute-start.4 = (bf16[160,960]{1,0:T(8,128)(2,1)}, bf16[160,960]{1,0:T(8,128)(2,1)S(1)}, u32[]{:S(2)}, u32[]{:S(2)}) collective-permute-start(bf16[160,960]{1,0:T(8,128)(2,1)} %collective-permute-done), channel_id=1, source_target_pairs={{0,4},{4,0},{8,12},{12,8},{16,20},{20,16},{24,28},{28,24},{1,5},{5... | collective-permute-start | bytes 921608 | tf_op jit(solution)/shard_map/ppermute | solution.py:55
  56.9 14.7 %collective-permute-start.5 = (bf16[160,960]{1,0:T(8,128)(2,1)}, bf16[160,960]{1,0:T(8,128)(2,1)S(1)}, u32[]{:S(2)}, u32[]{:S(2)}) collective-permute-start(bf16[160,960]{1,0:T(8,128)(2,1)} %collective-permute-done.1), channel_id=1, source_target_pairs={{0,4},{4,0},{8,12},{12,8},{16,20},{20,16},{24,28},{28,24},{1,5},{5... | collective-permute-start | bytes 921608 | tf_op jit(solution)/shard_map/ppermute | solution.py:55
  64.6 13.9 %collective-permute-start.6 = (bf16[160,960]{1,0:T(8,128)(2,1)}, bf16[160,960]{1,0:T(8,128)(2,1)S(1)}, u32[]{:S(2)}, u32[]{:S(2)}) collective-permute-start(bf16[160,960]{1,0:T(8,128)(2,1)} %collective-permute-done.2), channel_id=1, source_target_pairs={{0,4},{4,0},{8,12},{12,8},{16,20},{20,16},{24,28},{28,24},{1,5},{5... | collective-permute-start | bytes 921608 | tf_op jit(solution)/shard_map/ppermute | solution.py:55
  80.7 4.4 %copy-start.16 = (f32[1280]{0:T(1024)S(1)}, f32[1280]{0:T(1024)}, u32[]{:S(2)}) copy-start(f32[1280]{0:T(1024)} %param.13) | copy-start | bytes 15364
  85.2 2.4 copy-start.10
  87.5 15.3 %copy-start.3 = (bf16[2,512,5,64]{1,3,2,0:T(8,128)(2,1)}, bf16[2,512,5,64]{1,3,2,0:T(8,128)(2,1)S(1)}, u32[]{:S(2)}) copy-start(bf16[2,512,5,64]{1,3,2,0:T(8,128)(2,1)S(1)} %fusion.44) | copy-start | bytes 1966084
  95.3 5.7 %copy-start.8 = (f32[2,512,5,64]{1,3,2,0:T(8,128)S(1)}, f32[2,512,5,64]{1,3,2,0:T(8,128)}, u32[]{:S(2)}) copy-start(f32[2,512,5,64]{1,3,2,0:T(8,128)} %fusion.46) | copy-start | bytes 3932164
  95.3 41.6 %collective-permute-start.12 = (bf16[160,1792]{1,0:T(8,128)(2,1)}, bf16[160,1792]{1,0:T(8,128)(2,1)}, u32[]{:S(2)}, u32[]{:S(2)}) collective-permute-start(bf16[160,1792]{1,0:T(8,128)(2,1)} %bitcast.28), channel_id=1, source_target_pairs={{0,8},{4,12},{8,16},{12,20},{16,24},{20,28},{24,0},{28,4},{1,9},{5... | collective-permute-start | bytes 1720328 | tf_op jit(solution)/shard_map/ppermute | solution.py:49
  95.8 47.7 %collective-permute-start.13 = (bf16[160,1792]{1,0:T(8,128)(2,1)}, bf16[160,1792]{1,0:T(8,128)(2,1)}, u32[]{:S(2)}, u32[]{:S(2)}) collective-permute-start(bf16[160,1792]{1,0:T(8,128)(2,1)} %bitcast.28), channel_id=1, source_target_pairs={{0,16},{4,20},{8,24},{12,28},{16,0},{20,4},{24,8},{28,12},{1,17},{... | collective-permute-start | bytes 1720328 | tf_op jit(solution)/shard_map/ppermute | solution.py:49
  98.6 49.3 %collective-permute-start.14 = (bf16[160,1792]{1,0:T(8,128)(2,1)}, bf16[160,1792]{1,0:T(8,128)(2,1)}, u32[]{:S(2)}, u32[]{:S(2)}) collective-permute-start(bf16[160,1792]{1,0:T(8,128)(2,1)} %bitcast.28), channel_id=1, source_target_pairs={{0,24},{4,28},{8,0},{12,4},{16,8},{20,12},{24,16},{28,20},{1,25},{... | collective-permute-start | bytes 1720328 | tf_op jit(solution)/shard_map/ppermute | solution.py:49
  101.2 3.7 %copy-start.11 = (pred[2,512,512]{1,2,0:T(8,128)(4,1)S(1)}, pred[2,512,512]{1,2,0:T(8,128)(4,1)}, u32[]{:S(2)}) copy-start(pred[2,512,512]{1,2,0:T(8,128)(4,1)} %broadcast_and_fusion) | copy-start | bytes 1572868
  103.3 12.3 %collective-permute-start.10 = (bf16[152,1280]{1,0:T(8,128)(2,1)}, bf16[152,1280]{1,0:T(8,128)(2,1)S(1)}, u32[]{:S(2)}, u32[]{:S(2)}) collective-permute-start(bf16[152,1280]{1,0:T(8,128)(2,1)} %pad_maximum_fusion.10), channel_id=1, source_target_pairs={{0,4},{4,0},{8,12},{12,8},{16,20},{20,16},{24,28},{28,24},{1,5},{5... | collective-permute-start | bytes 1167368 | tf_op jit(solution)/shard_map/ppermute | solution.py:55
  103.7 16.7 %collective-permute-start.11 = (bf16[152,1280]{1,0:T(8,128)(2,1)}, bf16[152,1280]{1,0:T(8,128)(2,1)S(1)}, u32[]{:S(2)}, u32[]{:S(2)}) collective-permute-start(bf16[152,1280]{1,0:T(8,128)(2,1)} %collective-permute-done.7), channel_id=1, source_target_pairs={{0,4},{4,0},{8,12},{12,8},{16,20},{20,16},{24,28},{28,24},{1,5},{5... | collective-permute-start | bytes 1167368 | tf_op jit(solution)/shard_map/ppermute | solution.py:55
  115.6 12.9 %collective-permute-start.15 = (bf16[152,1280]{1,0:T(8,128)(2,1)}, bf16[152,1280]{1,0:T(8,128)(2,1)S(1)}, u32[]{:S(2)}, u32[]{:S(2)}) collective-permute-start(bf16[152,1280]{1,0:T(8,128)(2,1)} %collective-permute-done.8), channel_id=1, source_target_pairs={{0,4},{4,0},{8,12},{12,8},{16,20},{20,16},{24,28},{28,24},{1,5},{5... | collective-permute-start | bytes 1167368 | tf_op jit(solution)/shard_map/ppermute | solution.py:55
  120.3 16.6 %collective-permute-start.16 = (bf16[152,1280]{1,0:T(8,128)(2,1)}, bf16[152,1280]{1,0:T(8,128)(2,1)S(1)}, u32[]{:S(2)}, u32[]{:S(2)}) collective-permute-start(bf16[152,1280]{1,0:T(8,128)(2,1)} %collective-permute-done.9), channel_id=1, source_target_pairs={{0,4},{4,0},{8,12},{12,8},{16,20},{20,16},{24,28},{28,24},{1,5},{5... | collective-permute-start | bytes 1167368 | tf_op jit(solution)/shard_map/ppermute | solution.py:55
  148.0 13.8 %collective-permute-start.21 = (bf16[160,1792]{1,0:T(8,128)(2,1)}, bf16[160,1792]{1,0:T(8,128)(2,1)}, u32[]{:S(2)}, u32[]{:S(2)}) collective-permute-start(bf16[160,1792]{1,0:T(8,128)(2,1)} %bitcast.28), channel_id=1, source_target_pairs={{0,4},{4,0},{8,12},{12,8},{16,20},{20,16},{24,28},{28,24},{1,5},{5... | collective-permute-start | bytes 1720328 | tf_op jit(solution)/shard_map/ppermute | solution.py:55
  151.7 39.6 %all-to-all-start.2 = ((bf16[4,256,320]{1,2,0:T(8,128)(2,1)}), bf16[4,256,320]{1,2,0:T(8,128)(2,1)}, u32[]{:S(2)}, u32[]{:S(2)}) async-start(bf16[4,256,320]{1,2,0:T(8,128)(2,1)} %bitcast.193), calls=%async_computation.2 | async-start | bytes 1310720 | tf_op jit(solution)/shard_map/all_to_all | solution.py:223
  157.6 26.0 %collective-permute-start.17 = (bf16[8,40,1280]{2,1,0:T(8,128)(2,1)}, bf16[8,40,1280]{2,1,0:T(8,128)(2,1)S(1)}, u32[]{:S(2)}, u32[]{:S(2)}) collective-permute-start(bf16[8,40,1280]{2,1,0:T(8,128)(2,1)} %get-tuple-element.58), channel_id=1, source_target_pairs={{0,2},{1,3},{2,0},{3,1},{4,6},{5,7},{6,4},{7,5},{8,10},{9,11},{10,... | collective-permute-start | bytes 2457608 | tf_op jit(solution)/shard_map/ppermute | solution.py:41
  157.7 27.9 %collective-permute-start.22 = (bf16[160,1792]{1,0:T(8,128)(2,1)}, bf16[160,1792]{1,0:T(8,128)(2,1)S(1)}, u32[]{:S(2)}, u32[]{:S(2)}) collective-permute-start(bf16[160,1792]{1,0:T(8,128)(2,1)} %collective-permute-done.12), channel_id=1, source_target_pairs={{0,4},{4,0},{8,12},{12,8},{16,20},{20,16},{24,28},{28,24},{1,5},{5... | collective-permute-start | bytes 1720328 | tf_op jit(solution)/shard_map/ppermute | solution.py:55
  158.9 37.9 %collective-permute-start.23 = (bf16[160,1792]{1,0:T(8,128)(2,1)}, bf16[160,1792]{1,0:T(8,128)(2,1)}, u32[]{:S(2)}, u32[]{:S(2)}) collective-permute-start(bf16[160,1792]{1,0:T(8,128)(2,1)} %collective-permute-done.13), channel_id=1, source_target_pairs={{0,4},{4,0},{8,12},{12,8},{16,20},{20,16},{24,28},{28,24},{1,5},{5... | collective-permute-start | bytes 1720328 | tf_op jit(solution)/shard_map/ppermute | solution.py:55
  159.1 54.8 %collective-permute-start.24 = (bf16[160,1792]{1,0:T(8,128)(2,1)}, bf16[160,1792]{1,0:T(8,128)(2,1)}, u32[]{:S(2)}, u32[]{:S(2)}) collective-permute-start(bf16[160,1792]{1,0:T(8,128)(2,1)} %collective-permute-done.14), channel_id=1, source_target_pairs={{0,4},{4,0},{8,12},{12,8},{16,20},{20,16},{24,28},{28,24},{1,5},{5... | collective-permute-start | bytes 1720328 | tf_op jit(solution)/shard_map/ppermute | solution.py:55
  183.9 3.7 %collective-permute-start.18 = (bf16[2,8,40,1280]{3,2,1,0:T(8,128)(2,1)S(1)}, bf16[2,8,40,1280]{3,2,1,0:T(8,128)(2,1)S(1)}, u32[]{:S(2)}, u32[]{:S(2)}) collective-permute-start(bf16[2,8,40,1280]{3,2,1,0:T(8,128)(2,1)S(1)} %maximum_select_fusion.3), channel_id=1, source_target_pairs={{0,1},{1,0},{2,3},{3,2},{4,5},{5,4},{6,7},{7,6},{8,9},{9,8},{10,11... | collective-permute-start | bytes 4915208 | tf_op jit(solution)/shard_map/ppermute | solution.py:41
  186.7 2.1 copy-start.1
  189.3 7.5 %slice-start = ((s8[4587520]{0:T(1024)(128)(4,1)}), s8[393216]{0:T(1024)(128)(4,1)S(1)}, s32[]{:S(2)}) async-start(s8[4587520]{0:T(1024)(128)(4,1)} %bitcast.206), calls=%async_computation.3 | async-start | bytes 786432
  191.4 3.8 %copy-start.14 = (f32[1280]{0:T(1024)S(1)}, f32[1280]{0:T(1024)}, u32[]{:S(2)}) copy-start(f32[1280]{0:T(1024)} %param.14) | copy-start | bytes 15364
  191.4 5.4 %slice-start.1 = ((s8[4587520]{0:T(1024)(128)(4,1)}), s8[4194304]{0:T(1024)(128)(4,1)S(1)}, s32[]{:S(2)}) async-start(s8[4587520]{0:T(1024)(128)(4,1)} %bitcast.206), calls=%async_computation.4 | async-start | bytes 8388608
  195.3 16.4 %collective-permute-start.19 = (bf16[256,1280]{1,0:T(8,128)(2,1)S(1)}, bf16[256,1280]{1,0:T(8,128)(2,1)S(1)}, u32[]{:S(2)}, u32[]{:S(2)}) collective-permute-start(bf16[256,1280]{1,0:T(8,128)(2,1)S(1)} %multiply_convert_fusion.3), channel_id=1, source_target_pairs={{0,2},{1,3},{2,0},{3,1},{4,6},{5,7},{6,4},{7,5},{8,10},{9,11},{10,... | collective-permute-start | bytes 1966088 | tf_op jit(solution)/shard_map/ppermute | solution.py:41
  212.0 3.5 %collective-permute-start.20 = (bf16[2,256,1280]{2,1,0:T(8,128)(2,1)S(1)}, bf16[2,256,1280]{2,1,0:T(8,128)(2,1)S(1)}, u32[]{:S(2)}, u32[]{:S(2)}) collective-permute-start(bf16[2,256,1280]{2,1,0:T(8,128)(2,1)S(1)} %maximum_select_fusion.5), channel_id=1, source_target_pairs={{0,1},{1,0},{2,3},{3,2},{4,5},{5,4},{6,7},{7,6},{8,9},{9,8},{10,11... | collective-permute-start | bytes 3932168 | tf_op jit(solution)/shard_map/ppermute | solution.py:41
  215.1 2.6 copy-start.2
  217.6 2.8 copy-start.7
  229.0 14.2 %collective-permute-start.25 = (bf16[2,128,1280]{2,1,0:T(8,128)(2,1)S(1)}, bf16[2,128,1280]{2,1,0:T(8,128)(2,1)S(1)}, u32[]{:S(2)}, u32[]{:S(2)}) collective-permute-start(bf16[2,128,1280]{2,1,0:T(8,128)(2,1)S(1)} %dynamic-slice_bitcast_fusion.1), channel_id=1, source_target_pairs={{0,1},{1,0},{2,3},{3,2},{4,5},{5,4},{6,7},{7,6},{8,9},{9,8},{10,11... | collective-permute-start | bytes 1966088 | tf_op jit(solution)/shard_map/ppermute | solution.py:41
  241.6 4.2 %copy-start.9 = (bf16[512,1280]{1,0:T(8,128)(2,1)S(1)}, bf16[512,1280]{1,0:T(8,128)(2,1)}, u32[]{:S(2)}) copy-start(bf16[512,1280]{1,0:T(8,128)(2,1)} %convolution_convert_fusion) | copy-start | bytes 3932164
  242.9 3.0 %collective-permute-start.29 = (bf16[2,128,1280]{2,1,0:T(8,128)(2,1)S(1)}, bf16[2,128,1280]{2,1,0:T(8,128)(2,1)S(1)}, u32[]{:S(2)}, u32[]{:S(2)}) collective-permute-start(bf16[2,128,1280]{2,1,0:T(8,128)(2,1)S(1)} %dynamic-slice_bitcast_fusion), channel_id=1, source_target_pairs={{0,1},{1,0},{2,3},{3,2},{4,5},{5,4},{6,7},{7,6},{8,9},{9,8},{10,11... | collective-permute-start | bytes 1966088 | tf_op jit(solution)/shard_map/ppermute | solution.py:41
  244.4 1.5 copy-start.5
  244.4 9.1 %collective-permute-start.26 = (bf16[128,1280]{1,0:T(8,128)(2,1)S(1)}, bf16[128,1280]{1,0:T(8,128)(2,1)S(1)}, u32[]{:S(2)}, u32[]{:S(2)}) collective-permute-start(bf16[128,1280]{1,0:T(8,128)(2,1)S(1)} %fusion.42), channel_id=1, source_target_pairs={{0,2},{1,3},{2,0},{3,1},{4,6},{5,7},{6,4},{7,5},{8,10},{9,11},{10,... | collective-permute-start | bytes 983048 | tf_op jit(solution)/shard_map/ppermute | solution.py:41
  246.0 1.1 copy-start.6
  247.1 16.6 %copy-start.4 = (bf16[2,512,5,64]{1,3,2,0:T(8,128)(2,1)S(1)}, bf16[2,512,5,64]{1,3,2,0:T(8,128)(2,1)}, u32[]{:S(2)}) copy-start(bf16[2,512,5,64]{1,3,2,0:T(8,128)(2,1)} %copy-done.3) | copy-start | bytes 1966084
  247.9 12.7 %collective-permute-start.30 = (bf16[128,1280]{1,0:T(8,128)(2,1)}, bf16[128,1280]{1,0:T(8,128)(2,1)}, u32[]{:S(2)}, u32[]{:S(2)}) collective-permute-start(bf16[128,1280]{1,0:T(8,128)(2,1)} %fusion.43), channel_id=1, source_target_pairs={{0,2},{1,3},{2,0},{3,1},{4,6},{5,7},{6,4},{7,5},{8,10},{9,11},{10,... | collective-permute-start | bytes 983048 | tf_op jit(solution)/shard_map/ppermute | solution.py:41
  253.5 0.7 copy-start.12
  262.3 8.2 %collective-permute-start.31 = (bf16[128,1280]{1,0:T(8,128)(2,1)S(1)}, bf16[128,1280]{1,0:T(8,128)(2,1)}, u32[]{:S(2)}, u32[]{:S(2)}) collective-permute-start(bf16[128,1280]{1,0:T(8,128)(2,1)S(1)} %get-tuple-element.69), channel_id=1, source_target_pairs={{0,2},{1,3},{2,0},{3,1},{4,6},{5,7},{6,4},{7,5},{8,10},{9,11},{10,... | collective-permute-start | bytes 983048 | tf_op jit(solution)/shard_map/ppermute | solution.py:41
  264.5 13.0 %collective-permute-start.27 = (bf16[128,1280]{1,0:T(8,128)(2,1)S(1)}, bf16[128,1280]{1,0:T(8,128)(2,1)S(1)}, u32[]{:S(2)}, u32[]{:S(2)}) collective-permute-start(bf16[128,1280]{1,0:T(8,128)(2,1)S(1)} %get-tuple-element.68), channel_id=1, source_target_pairs={{0,2},{1,3},{2,0},{3,1},{4,6},{5,7},{6,4},{7,5},{8,10},{9,11},{10,... | collective-permute-start | bytes 983048 | tf_op jit(solution)/shard_map/ppermute | solution.py:41
  271.7 9.3 %collective-permute-start.32 = (bf16[2,128,1280]{2,1,0:T(8,128)(2,1)S(1)}, bf16[2,128,1280]{2,1,0:T(8,128)(2,1)S(1)}, u32[]{:S(2)}, u32[]{:S(2)}) collective-permute-start(bf16[2,128,1280]{2,1,0:T(8,128)(2,1)S(1)} %maximum_select_fusion.10), channel_id=1, source_target_pairs={{0,1},{1,0},{2,3},{3,2},{4,5},{5,4},{6,7},{7,6},{8,9},{9,8},{10,11... | collective-permute-start | bytes 1966088 | tf_op jit(solution)/shard_map/ppermute | solution.py:41
  277.5 3.9 %collective-permute-start.28 = (bf16[2,128,1280]{2,1,0:T(8,128)(2,1)S(1)}, bf16[2,128,1280]{2,1,0:T(8,128)(2,1)S(1)}, u32[]{:S(2)}, u32[]{:S(2)}) collective-permute-start(bf16[2,128,1280]{2,1,0:T(8,128)(2,1)S(1)} %maximum_select_fusion.8), channel_id=1, source_target_pairs={{0,1},{1,0},{2,3},{3,2},{4,5},{5,4},{6,7},{7,6},{8,9},{9,8},{10,11... | collective-permute-start | bytes 1966088 | tf_op jit(solution)/shard_map/ppermute | solution.py:41
